TPU v7x, 256 devices: a whole 4x4x8 slice. The times are simulated.
256 devices in a mesh: seq: 64 (over y_lo, x, z), tile: 4 (over y_hi, core).
Axes of the slice: x: 4, y: 4 (y_hi: 2, y_lo: 2; y = y_hi * 2 + y_lo), z: 8, core: 2. Of those that a mesh axis runs over, the one named last changes fastest.
Arguments:
- queries: bfloat16 [16384, 512], P('seq', 'tile'), may hold values from -6 to 6
- keys: bfloat16 [16384, 512], P('seq', 'tile'), may hold values from -6 to 6
- values: bfloat16 [16384, 512], P('seq', 'tile'), may hold values from -6 to 6
- attn_out: bfloat16 [16384, 512], P('seq', 'tile'), may hold values from -6 to 6
- log_norm: float32 [8, 16384], P('tile', 'seq'), as said below
- upstream: bfloat16 [16384, 1024], P('seq', 'tile'), may hold values from -6 to 6
- dec_grad: bfloat16 [16384, 1024], P('seq', 'tile'), may hold values from -6 to 6
- w_dec: bfloat16 [1024, 1024], P(None, 'tile'), may hold values from -0.1875 to 0.1875
- w_out: bfloat16 [512, 1024], P('tile'), may hold values from -0.375 to 0.375
- block_order: int32 [64, 64], P('seq'), may hold values from 0 to 63, each once within a row
Outputs:
- grad_queries: bfloat16 [16384, 512], P('seq', 'tile')
- grad_keys: bfloat16 [16384, 512], P('seq', 'tile')
- grad_values: bfloat16 [16384, 512], P('seq', 'tile')
Inputs may be any that keep to these rules, and one draw needn't show every extreme that they name: Row k of block_order is a permutation of the 64 token blocks of index k along seq; entry d names the block that the decoder tile of index d along seq holds as its k-th block. Every entry of log_norm lies between ln(16384) - 0.2 and ln(16384) + 1.2.
All inputs are finite; a program needn't handle non-finite values.
Results may differ from a plain program's by a relative error of at most 0.025.
Values may be sent and summed in bfloat16 or wider, within the bound.
No kernel may reach another device: no remote copies, remote signals or barrier semaphores. Data moves between devices by JAX's collectives and lax.ppermute only.
A program may use at most 128 MiB of HBM per device.

v0:
```python
import math

import jax
import jax.numpy as jnp
from jax import lax
from jax.sharding import PartitionSpec as P

HD = 64


def query_terms(query_blk, grad_blk, norm_blk, delta_blk, key_blk, value_blk):
    score_scale = 1.0 / math.sqrt(HD)
    scores = (
        jnp.einsum("qhd,khd->hqk", query_blk, key_blk, preferred_element_type=jnp.float32)
        * score_scale
    )
    attn_probs = jnp.exp(scores - norm_blk[:, :, None])
    d_probs = jnp.einsum("qhd,khd->hqk", grad_blk, value_blk, preferred_element_type=jnp.float32)
    d_scores = (attn_probs * (d_probs - delta_blk[:, :, None])).astype(jnp.bfloat16)
    return jnp.einsum("hqk,khd->qhd", d_scores, key_blk, preferred_element_type=jnp.float32)


def key_terms(query_blk, grad_blk, norm_blk, delta_blk, key_blk, value_blk):
    score_scale = 1.0 / math.sqrt(HD)
    scores = (
        jnp.einsum("qhd,khd->hqk", query_blk, key_blk, preferred_element_type=jnp.float32)
        * score_scale
    )
    attn_probs = jnp.exp(scores - norm_blk[:, :, None])
    probs_half = attn_probs.astype(jnp.bfloat16)
    grad_v = jnp.einsum("hqk,qhd->khd", probs_half, grad_blk, preferred_element_type=jnp.float32)
    d_probs = jnp.einsum("qhd,khd->hqk", grad_blk, value_blk, preferred_element_type=jnp.float32)
    d_scores = (attn_probs * (d_probs - delta_blk[:, :, None])).astype(jnp.bfloat16)
    grad_k = jnp.einsum("hqk,qhd->khd", d_scores, query_blk, preferred_element_type=jnp.float32)
    return (grad_k, grad_v)


def body(queries, keys, values, attn_out, log_norm, upstream, dec_grad, w_dec, w_out, block_order):
    tok_count = queries.shape[0]
    head_count = queries.shape[1] // HD
    feature_width = queries.shape[1]
    score_scale = 1.0 / math.sqrt(HD)
    partial_rows = lax.dot_general(
        dec_grad, w_dec, (((1,), (1,)), ((), ())), preferred_element_type=jnp.float32
    )
    summed = lax.psum_scatter(partial_rows, "tile", scatter_dimension=1, tiled=True).astype(
        jnp.bfloat16
    )
    shard_count = lax.axis_size("seq")
    arrived = lax.all_to_all(summed, "seq", split_axis=0, concat_axis=0, tiled=True)
    pieces = arrived.reshape(shard_count, tok_count // shard_count, summed.shape[1])
    inverse = jnp.argsort(block_order[0])
    skip_grad = jnp.take(pieces, inverse, axis=0).reshape(summed.shape)
    total_grad = (upstream.astype(jnp.float32) + skip_grad.astype(jnp.float32)).astype(jnp.bfloat16)
    d_attn = lax.dot_general(
        lax.all_gather(total_grad, "tile", axis=1, tiled=True),
        w_out,
        (((1,), (1,)), ((), ())),
        preferred_element_type=jnp.float32,
    ).astype(jnp.bfloat16)
    query_heads = queries.reshape(tok_count, head_count, HD)
    grad_heads = d_attn.reshape(tok_count, head_count, HD)
    output_heads = attn_out.reshape(tok_count, head_count, HD)
    key_heads = keys.reshape(tok_count, head_count, HD)
    value_heads = values.reshape(tok_count, head_count, HD)
    row_delta = jnp.sum(grad_heads.astype(jnp.float32) * output_heads.astype(jnp.float32), axis=2).T
    key_blk = lax.all_gather(keys, "seq", axis=0, tiled=True)
    value_blk = lax.all_gather(values, "seq", axis=0, tiled=True)
    row_count = key_blk.shape[0]
    grad_q = query_terms(
        query_heads,
        grad_heads,
        log_norm,
        row_delta,
        key_blk.reshape(row_count, head_count, HD),
        value_blk.reshape(row_count, head_count, HD),
    )
    all_norms, all_deltas = (
        lax.all_gather(log_norm.T, "seq", axis=0, tiled=True),
        lax.all_gather(row_delta.T, "seq", axis=0, tiled=True),
    )
    query_blk = lax.all_gather(queries, "seq", axis=0, tiled=True)
    grad_blk = lax.all_gather(d_attn, "seq", axis=0, tiled=True)
    row_count = query_blk.shape[0]
    norm_blk = all_norms.T
    delta_blk = all_deltas.T
    grad_k, grad_v = key_terms(
        query_blk.reshape(row_count, head_count, HD),
        grad_blk.reshape(row_count, head_count, HD),
        norm_blk,
        delta_blk,
        key_heads,
        value_heads,
    )
    grad_k, grad_v = (grad_k, grad_v)
    grad_k = grad_k.reshape(tok_count, feature_width)
    grad_v = grad_v.reshape(tok_count, feature_width)
    grad_queries = (grad_q * score_scale).reshape(tok_count, feature_width).astype(jnp.bfloat16)
    grad_keys = (grad_k * score_scale).astype(jnp.bfloat16)
    grad_values = grad_v.astype(jnp.bfloat16)
    return (grad_queries, grad_keys, grad_values)


def solution(mesh):
    return jax.shard_map(
        body,
        mesh=mesh,
        in_specs=(
            P("seq", "tile"),
            P("seq", "tile"),
            P("seq", "tile"),
            P("seq", "tile"),
            P("tile", "seq"),
            P("seq", "tile"),
            P("seq", "tile"),
            P(None, "tile"),
            P("tile", None),
            P("seq", None),
        ),
        out_specs=(P("seq", "tile"), P("seq", "tile"), P("seq", "tile")),
        check_vma=False,
    )
```

profile of v0, /device:TPU:2, one launch (start us, length us, event | category | flops | bytes accessed | tf_op | source)
XLA Modules:
  0.0 1153.7 jit_solution(16210075738116967193)
XLA Ops:
  8.0 0.0 copy-start
  8.0 0.0 reduce-scatter.2.cloned.1.call-start
  8.1 1.0 copy-done
  9.0 2.2 fusion.14
  11.3 0.0 reduce-scatter.2.cloned.1.call-update
  11.3 0.0 all-gather.5.cloned.1.call-start
  11.3 0.5 all-gather.5.cloned.1.call-update
  11.9 0.0 all-gather.7.cloned.1.call-start
  11.9 1.6 copy.22
  13.5 0.0 all-gather.7.cloned.1.call-update
  13.5 0.0 all-gather.9.cloned.1.call-start
  13.6 0.5 all-gather.9.cloned.1.call-update
  14.1 0.9 copy.23
  15.0 2.7 sort.17
  17.7 0.1 broadcast_in_dim.20
  17.8 0.1 broadcast_in_dim.21
  17.9 33.7 %reduce-scatter.2.cloned.1.call-done = f32[256,256]{1,0:T(8,128)} async-done(((f32[256,1024]{1,0:T(8,128)}), f32[256,256]{1,0:T(8,128)}) %reduce-scatter.2.cloned.1.call-update) | async-done | bytes 262160 | tf_op jit(solution)/shard_map/reduce_scatter | solution.py:46
  51.6 1.0 convert_element_type.61
  52.6 0.7 all_to_all.6
  53.3 10.6 all-to-all-start
  63.8 0.0 all-gather.11.cloned.1.call-start
  63.9 10.0 all-to-all-done
  73.9 0.7 gather_fusion
  74.6 1.0 add_convert_fusion
  75.7 8.0 all_gather.22
  83.7 1.9 fusion.10
  85.6 0.0 all-gather.11.cloned.1.call-update
  85.6 0.9 copy.20
  86.5 0.9 copy.25
  87.5 138.4 %all_gather.25 = f32[16384,2]{0,1:T(2,128)S(1)} all-gather(f32[256,2]{0,1:T(2,128)} %bitcast.78), channel_id=1, replica_groups=mesh['seq'=64,'tile'=4] {'seq'}, dimensions={0}, use_global_device_ids=true | all-gather | bytes 133120 | tf_op jit(solution)/shard_map/all_gather | solution.py:79
  225.9 151.1 %all_gather.27 = f32[16384,2]{0,1:T(2,128)S(1)} all-gather(f32[256,2]{0,1:T(2,128)S(1)} %get-tuple-element.11), channel_id=1, replica_groups=mesh['seq'=64,'tile'=4] {'seq'}, dimensions={0}, use_global_device_ids=true | all-gather | bytes 133120 | tf_op jit(solution)/shard_map/all_gather | solution.py:80
  377.0 0.0 all-gather.5.cloned.1.call-done
  377.0 6.4 copy.21
  383.4 0.0 copy-start.5
  383.4 0.0 copy-start.6
  383.4 15.4 %fusion.13 = f32[2,256,16384]{2,1,0:T(8,128)} fusion(bf16[256,2,64]{0,2,1:T(8,128)(2,1)S(1)} %bitcast.74, bf16[16384,2,64]{0,2,1:T(8,128)(2,1)} %bitcast.65), kind=kOutput, calls=%fused_computation.21 | convolution fusion | flops 1073741824 | bytes 37814272 | tf_op jit(solution)/shard_map/qhd,khd->hqk/dot_general | solution.py:14
  398.8 165.3 %all-gather.7.cloned.1.call-done = bf16[16384,128]{0,1:T(8,128)(2,1)} async-done(((bf16[256,128]{0,1:T(8,128)(2,1)}), bf16[16384,128]{0,1:T(8,128)(2,1)}) %all-gather.7.cloned.1.call-update) | async-done | bytes 4194320 | tf_op jit(solution)/shard_map/all_gather | solution.py:68
  564.1 0.0 copy-done.5
  564.1 0.0 copy-done.6
  564.1 18.0 %fusion.5 = bf16[2,256,64]{1,2,0:T(8,128)(2,1)S(1)} fusion(bf16[16384,2,64]{0,2,1:T(8,128)(2,1)} %bitcast.66, f32[2,256,16384]{2,1,0:T(8,128)} %fusion.13, bf16[256,2,64]{0,2,1:T(8,128)(2,1)S(1)} %bitcast.75, bf16[16384,2,64]{0,2,1:T(8,128)(2,1)} %bitcast.79, f32[2,256]{1,0:T(2,128)S(1)} %bitcast.77, f32[2,256]{1,0:T(2,128)S(1)} %copy-done.6), kind=kOutput, calls=%fused_computation.9 | convolution fusion | flops 2189492224 | bytes 42078208 | tf_op jit(solution)/shard_map/hqk,khd->qhd/dot_general | solution.py:20
  582.1 0.7 copy.27
  582.8 275.7 %all-gather.9.cloned.1.call-done = bf16[16384,128]{1,0:T(8,128)(2,1)} async-done(((bf16[256,128]{1,0:T(8,128)(2,1)}), bf16[16384,128]{1,0:T(8,128)(2,1)}) %all-gather.9.cloned.1.call-update) | async-done | bytes 4194320 | tf_op jit(solution)/shard_map/all_gather | solution.py:82
  858.5 6.4 copy.24
  864.9 17.8 %fusion.15 = f32[2,16384,256]{2,1,0:T(8,128)} fusion(bf16[16384,2,64]{0,2,1:T(8,128)(2,1)} %bitcast.61, bf16[256,2,64]{0,2,1:T(8,128)(2,1)S(1)} %bitcast.73), kind=kOutput, calls=%fused_computation.23 | convolution fusion | flops 1073741824 | bytes 37814272 | tf_op jit(solution)/shard_map/qhd,khd->hqk/dot_general | solution.py:26
  882.7 229.8 %all-gather.11.cloned.1.call-done = bf16[16384,128]{0,1:T(8,128)(2,1)} async-done(((bf16[256,128]{0,1:T(8,128)(2,1)}), bf16[16384,128]{0,1:T(8,128)(2,1)}) %all-gather.11.cloned.1.call-update) | async-done | bytes 4194320 | tf_op jit(solution)/shard_map/all_gather | solution.py:83
  1112.5 0.0 copy-start.3
  1112.5 0.0 copy-start.4
  1112.5 14.8 %fusion.7 = bf16[2,64,256]{2,1,0:T(8,128)(2,1)S(1)} fusion(bf16[16384,2,64]{0,2,1:T(8,128)(2,1)} %bitcast.63, f32[2,16384,256]{2,1,0:T(8,128)} %fusion.15, f32[2,16384]{1,0:T(2,128)S(1)} %bitcast.67), kind=kOutput, calls=%fused_computation.11 | convolution fusion | flops 1098940416 | bytes 37945344 | tf_op jit(solution)/shard_map/hqk,qhd->khd/dot_general | solution.py:31
  1127.3 0.0 copy-done.3
  1127.3 0.0 copy-done.4
  1127.3 0.0 copy-start.2
  1127.3 0.0 copy-start.1
  1127.4 14.5 %fusion.49 = bf16[2,16384,256]{2,1,0:T(8,128)(2,1)S(1)} fusion(f32[2,16384]{1,0:T(2,128)S(1)} %bitcast.69, bf16[256,2,64]{0,2,1:T(8,128)(2,1)S(1)} %bitcast.72, bf16[16384,2,64]{0,2,1:T(8,128)(2,1)S(1)} %bitcast.64, f32[2,16384]{1,0:T(2,128)S(1)} %bitcast.68, f32[2,16384,256]{2,1,0:T(8,128)} %fusion.15), kind=kOutput, calls=%bitcast_fusion.10.clone.1 | convolution fusion | flops 1115684864 | bytes 54853632 | tf_op jit(solution)/shard_map/qhd,khd->hqk/dot_general | solution.py:32
  1141.8 0.0 copy-done.2
  1141.8 2.8 fusion.6
  1144.7 0.7 copy.28
  1145.4 0.7 copy.29
  1146.1 0.0 copy-done.1
  (5 shorter events, 0.1 us)
Async XLA Ops:
  8.0 1.1 copy-start
  8.0 43.6 %reduce-scatter.2.cloned.1.call-start = ((), (), s32[]{:S(2)}) async-start(), calls=%async_computation.3 | async-start | bytes 1310720 | tf_op jit(solution)/shard_map/reduce_scatter | solution.py:46
  11.3 365.7 %all-gather.5.cloned.1.call-start = ((), (), s32[]{:S(2)}) async-start(), calls=%async_computation.2 | async-start | bytes 4259840 | tf_op jit(solution)/shard_map/all_gather | solution.py:67
  11.9 552.2 %all-gather.7.cloned.1.call-start = ((), (), s32[]{:S(2)}) async-start(), calls=%async_computation.4 | async-start | bytes 4259840 | tf_op jit(solution)/shard_map/all_gather | solution.py:68
  13.5 845.0 %all-gather.9.cloned.1.call-start = ((), (), s32[]{:S(2)}) async-start(), calls=%async_computation.5 | async-start | bytes 4259840 | tf_op jit(solution)/shard_map/all_gather | solution.py:82
  53.3 20.6 %all-to-all-start = ((bf16[64,4,256]{2,1,0:T(4,128)(2,1)}), bf16[64,4,256]{2,1,0:T(4,128)(2,1)S(1)}, u32[]{:S(2)}, u32[]{:S(2)}) async-start(bf16[64,4,256]{2,1,0:T(4,128)(2,1)} %all_to_all.6), calls=%async_computation.1 | async-start | bytes 262144 | tf_op jit(solution)/shard_map/all_to_all | solution.py:50
  63.8 1048.6 %all-gather.11.cloned.1.call-start = ((), (), s32[]{:S(2)}) async-start(), calls=%async_computation.6 | async-start | bytes 4259840 | tf_op jit(solution)/shard_map/all_gather | solution.py:83
  383.4 180.7 %copy-start.5 = (bf16[256,128]{0,1:T(8,128)(2,1)S(1)}, bf16[256,128]{0,1:T(8,128)(2,1)}, u32[]{:S(2)}) copy-start(bf16[256,128]{0,1:T(8,128)(2,1)} %get-tuple-element.12) | copy-start | bytes 196612
  383.4 180.7 %copy-start.6 = (f32[2,256]{1,0:T(2,128)S(1)}, f32[2,256]{1,0:T(2,128)}, u32[]{:S(2)}) copy-start(f32[2,256]{1,0:T(2,128)} %param.14) | copy-start | bytes 6148
  1112.5 14.8 %copy-start.3 = (bf16[16384,128]{0,1:T(8,128)(2,1)S(1)}, bf16[16384,128]{0,1:T(8,128)(2,1)}, u32[]{:S(2)}) copy-start(bf16[16384,128]{0,1:T(8,128)(2,1)} %all-gather.11.cloned.1.call-done) | copy-start | bytes 12582916
  1112.5 14.8 %copy-start.4 = (bf16[256,128]{0,1:T(8,128)(2,1)S(1)}, bf16[256,128]{0,1:T(8,128)(2,1)}, u32[]{:S(2)}) copy-start(bf16[256,128]{0,1:T(8,128)(2,1)} %copy.22) | copy-start | bytes 196612
  1127.3 14.5 %copy-start.2 = (bf16[16384,128]{0,1:T(8,128)(2,1)S(1)}, bf16[16384,128]{0,1:T(8,128)(2,1)}, u32[]{:S(2)}) copy-start(bf16[16384,128]{0,1:T(8,128)(2,1)} %copy.24) | copy-start | bytes 12582916
  1127.3 18.8 %copy-start.1 = (bf16[1024,256]{1,0:T(8,128)(2,1)S(1)}, bf16[1024,256]{1,0:T(8,128)(2,1)}, u32[]{:S(2)}) copy-start(bf16[1024,256]{1,0:T(8,128)(2,1)} %param.17) | copy-start | bytes 1572868
Sparse Core Ops, SparseCore 0:
  11.6 39.9 reduce-scatter.1
Sparse Core Ops, SparseCore 1:
  13.5 296.6 all-gather.4
  312.5 251.5 all-gather.6
  565.9 292.6 all-gather.8
  860.9 251.5 all-gather.10
where the time goes:
time: 1160 us; the launch traced here: 1150 us
  waiting for transfers between devices  715 us (62%)
  blocking collectives  297 us (26%)
  matrix products  87.4 us (8%)
  local copies, waits for them, and re-layouts  22 us (2%)
  between operations  15.8 us (1%)
    all_gather x1, waiting for transfers between devices, body(): query_blk = lax.all_gather(queries, 'seq', axis=0, tiled=True)  276 us
    all_gather x1, waiting for transfers between devices, body(): grad_blk = lax.all_gather(d_attn, 'seq', axis=0, tiled=True)  230 us
    all_gather x1, waiting for transfers between devices, body(): value_blk = lax.all_gather(values, 'seq', axis=0, tiled=True)  165 us
    all_gather x1, blocking collectives, body(): lax.all_gather(row_delta.T, 'seq', axis=0, tiled=True)  151 us
    all_gather x1, blocking collectives, body(): lax.all_gather(log_norm.T, 'seq', axis=0, tiled=True)  138 us
    reduce_scatter x1, waiting for transfers between devices, body(): lax.psum_scatter(partial_rows, 'tile', scatter_dimension=1, tiled=True)  33.7 us
  transfers between devices with their start and end apart: 6, of which 5 were waited for; matrix products, arithmetic and copies ran while one was open for 7% of the time, Pallas kernels for 0%

commit v1 on v0

v1 whole, which is shorter than its diff:
```python
import jax
import jax.numpy as jnp
from jax import lax
from jax.experimental import pallas as pl
from jax.experimental.pallas import tpu as pltpu
from jax.sharding import Mesh
from jax.sharding import PartitionSpec as P

HD = 64
BLK = 4
SIDE = 8
PAIR = 2
RING = (0, 1, 2, 3, 4, -1, -2, -3)
VMEM = 24 << 20
LARGE = 60 << 20
R = ("yl", "x")
C = "z"
S = ("yl", "x", "z")
T = ("yh", "core")

f32 = jnp.float32
bf16 = jnp.bfloat16


def nt(a, b):
    return lax.dot_general(a, b, (((1,), (1,)), ((), ())), preferred_element_type=f32)


def nn(a, b):
    return lax.dot_general(a, b, (((1,), (0,)), ((), ())), preferred_element_type=f32)


def swap_blocks(x):
    rows = x.shape[0]
    out = lax.broadcasted_iota(jnp.int32, (rows, rows), 0)
    src = lax.broadcasted_iota(jnp.int32, (rows, rows), 1)
    pick = ((out >> 2) & 7) * 32 + (out >> 5) * 4 + (out & 3)
    return nn((src == pick).astype(f32).astype(bf16), x).astype(bf16)


def project_kernel(tile_ref, *refs):
    ins, part_ref, u_refs, copied, sems = refs[:7], refs[7], refs[8:12], refs[12:16], refs[16]
    dec_ref, up_ref, w_dec_ref, w_ref = copied
    outs = [dec_ref, up_ref, w_dec_ref] + [w_ref.at[i * 128 : (i + 1) * 128] for i in range(4)]
    copies = [pltpu.make_async_copy(src, dst, sems.at[i]) for i, (src, dst) in enumerate(zip(ins, outs))]
    for copy in copies:
        copy.start()
    copies[0].wait()
    dec = swap_blocks(dec_ref[...])
    for copy in copies[1:]:
        copy.wait()
    w = nn(w_ref[...], w_dec_ref[...]).astype(bf16)
    part = nt(dec, w).astype(bf16)
    columns = pl.ds(pl.multiple_of(tile_ref[0] * 256, 256), 256)
    u = nt(up_ref[...], w_ref[:, columns]).astype(bf16)
    for i in range(4):
        part_ref[tile_ref[0] ^ i] = part[:, i * 128 : (i + 1) * 128]
        u_refs[i][...] = u[:, i * 128 : (i + 1) * 128]


def project(tile, dec, up, w_dec, w_outs):
    out = pl.pallas_call(
        project_kernel,
        in_specs=[pl.BlockSpec(memory_space=pltpu.SMEM)] + [pl.BlockSpec(memory_space=pl.ANY)] * 7,
        out_shape=[jax.ShapeDtypeStruct((4, 256, 128), bf16)]
        + [jax.ShapeDtypeStruct((256, 128), bf16)] * 4,
        scratch_shapes=[
            pltpu.VMEM(dec.shape, bf16),
            pltpu.VMEM(up.shape, bf16),
            pltpu.VMEM(w_dec.shape, bf16),
            pltpu.VMEM((512, 1024), bf16),
            pltpu.SemaphoreType.DMA((7,)),
        ],
        compiler_params=pltpu.CompilerParams(vmem_limit_bytes=LARGE),
        name="project",
    )(tile, dec, up, w_dec, *w_outs)
    return out[0], out[1:]


def pack_kernel(part_ref, q_ref, out_ref, misc_ref, u0_ref, u1_ref, u2_ref, u3_ref, pay_ref):
    u = u0_ref[...].astype(f32)
    for u_ref in (u1_ref, u2_ref, u3_ref):
        u += u_ref[...].astype(f32)
    u = u.astype(bf16)
    total = part_ref[0].astype(f32)
    for t in range(1, 4):
        total += part_ref[t].astype(f32)
    skip = swap_blocks(total.astype(bf16))
    for r in range(SIDE):
        pay_ref[r, 0:256] = q_ref[...]
        pay_ref[r, 256:512] = out_ref[...]
        pay_ref[r, 512:768] = u
        pay_ref[r, 768:1024] = skip
        pay_ref[r, 1024:1040] = misc_ref[...]


def pack(part, q, out, misc, us):
    return pl.pallas_call(
        pack_kernel,
        out_shape=jax.ShapeDtypeStruct((SIDE, 1040, 128), bf16),
        compiler_params=pltpu.CompilerParams(vmem_limit_bytes=VMEM),
        name="pack",
    )(part, q, out, misc, *us)


def head_masks():
    lane = lax.broadcasted_iota(jnp.int32, (1, 128), 1)
    return [(lane < HD).astype(f32).astype(bf16), (lane >= HD).astype(f32).astype(bf16)]


def token_grads(pay_ref, r):
    rows = 256
    misc = pay_ref[r, 1024:1040].astype(f32)
    dest = jnp.concatenate([misc[12:13], misc[13:14]], 1).astype(jnp.int32)
    token = lax.broadcasted_iota(jnp.int32, (rows, rows), 0)
    place = (token == dest).astype(f32).astype(bf16)
    arrived = pay_ref[:, pl.ds(pl.multiple_of(768 + r * 32, 32), 32)].reshape(rows, 128)
    d_out = (nn(place, arrived) + pay_ref[r, 512:768].astype(f32)).astype(bf16)
    prod = d_out.astype(f32) * pay_ref[r, 256:512].astype(f32)
    hi = prod.astype(bf16)
    rest = prod - hi.astype(f32)
    mid = rest.astype(bf16)
    low = (rest - mid.astype(f32)).astype(bf16)
    sub8 = lax.broadcasted_iota(jnp.int32, (8, 128), 0)
    lane8 = lax.broadcasted_iota(jnp.int32, (8, 128), 1)
    head_rows = (sub8 == lane8 // HD).astype(f32).astype(bf16)
    return d_out, nt(head_rows, hi) + nt(head_rows, mid) + nt(head_rows, low)


def attention_kernel(place_ref, pay_ref, *refs):
    kv_refs = refs[:SIDE]
    dq_ref, vk_ref, kt_ref, dv_acc, dk_acc = refs[SIDE:]
    dv_acc[...] = jnp.zeros_like(dv_acc)
    dk_acc[...] = jnp.zeros_like(dk_acc)
    for t in range(SIDE):
        kt_ref[:, t * 256 : (t + 1) * 256] = kv_refs[t][:, 0:128].astype(f32).T.astype(bf16)

    def step_of(step, carry):
        attention_step(step, place_ref, pay_ref, kv_refs, kt_ref, dq_ref, dv_acc, dk_acc)
        return carry

    lax.fori_loop(0, SIDE // PAIR, step_of, 0)
    for t in range(SIDE):
        c = (place_ref[1] - RING[t]) & (SIDE - 1)
        vk_ref[c, 0] = dv_acc[t * 256 : (t + 1) * 256, :].astype(bf16)
        vk_ref[c, 1] = dk_acc[t * 256 : (t + 1) * 256, :].astype(bf16)


def attention_step(step, place_ref, pay_ref, kv_refs, kt_ref, dq_ref, dv_acc, dk_acc):
    masks = head_masks()
    chains = []
    for i in range(PAIR):
        r = step * PAIR + i
        d_out, delta = token_grads(pay_ref, r)
        query = pay_ref[r, 0:256] * bf16(0.125)
        misc = pay_ref[r, 1024:1040].astype(f32)
        parts = misc[0:4] + misc[4:8] + misc[8:12]
        for h in range(2):
            norm = jnp.concatenate([parts[2 * h : 2 * h + 1], parts[2 * h + 1 : 2 * h + 2]], 1)
            chains.append((h, query * masks[h], d_out * masks[h], norm, delta[h : h + 1, :]))
    queries = jnp.concatenate([chain[1] for chain in chains], 0)
    grads = jnp.concatenate([chain[2] for chain in chains], 0)

    def scores_of(t):
        key, value = kv_refs[t][:, 0:128], kv_refs[t][:, 128:256]
        return [(nt(key, query), nt(value, grad)) for _, query, grad, _, _ in chains]

    dq = [jnp.zeros((HD, 256), f32) for _ in chains]
    later = scores_of(0)
    for t in range(SIDE):
        now = later
        if t + 1 < SIDE:
            later = scores_of(t + 1)
        keys = slice(t * 256, (t + 1) * 256)
        probs, d_scores = [], []
        for i, (h, _, _, norm, delta) in enumerate(chains):
            scores, d_probs = now[i]
            p = jnp.exp(scores - norm)
            d_scores.append((p * (d_probs - delta)).astype(bf16))
            probs.append(p.astype(bf16))
            dq[i] += nn(kt_ref[h * HD : (h + 1) * HD, keys], d_scores[i])
        dv_acc[keys, :] += nn(jnp.concatenate(probs, 1), grads)
        dk_acc[keys, :] += nn(jnp.concatenate(d_scores, 1), queries)
    for i in range(PAIR):
        both = jnp.concatenate(dq[2 * i : 2 * i + 2], 0)
        dq_ref[(step * PAIR + i) ^ place_ref[0]] = (both * 0.125).astype(bf16)


def attention(place, pay, ring):
    dq_shape, vk_shape = (SIDE, 128, 256), (SIDE, 2, 256, 128)
    return pl.pallas_call(
        attention_kernel,
        in_specs=[pl.BlockSpec(memory_space=pltpu.SMEM)] + [pl.BlockSpec(memory_space=pltpu.VMEM)] * 9,
        out_shape=[jax.ShapeDtypeStruct(dq_shape, bf16), jax.ShapeDtypeStruct(vk_shape, bf16)],
        scratch_shapes=[
            pltpu.VMEM((128, SIDE * 256), bf16),
            pltpu.VMEM((SIDE * 256, 128), f32),
            pltpu.VMEM((SIDE * 256, 128), f32),
        ],
        compiler_params=pltpu.CompilerParams(vmem_limit_bytes=VMEM),
        cost_estimate=pl.CostEstimate(flops=20 << 30, bytes_accessed=1 << 23, transcendentals=1 << 23),
        name="attention",
    )(place, pay, *ring)


def finish_kernel(vk_ref, *refs):
    dq_refs, (dq_ref, dk_ref, dv_ref) = refs[:SIDE], refs[SIDE:]

    def total(parts):
        out = parts[0].astype(f32)
        for part in parts[1:]:
            out += part.astype(f32)
        return out

    dq_ref[...] = total([ref[...] for ref in dq_refs]).T.astype(bf16)
    dv_ref[...] = total([vk_ref[i, 0] for i in range(SIDE)]).astype(bf16)
    dk_ref[...] = total([vk_ref[i, 1] for i in range(SIDE)]).astype(bf16)


finish_call = pl.pallas_call(
    finish_kernel,
    out_shape=[jax.ShapeDtypeStruct((256, 128), bf16)] * 3,
    compiler_params=pltpu.CompilerParams(vmem_limit_bytes=VMEM),
    name="finish",
)


def body(queries, keys, values, attn_out, log_norm, upstream, dec_grad, w_dec, w_out, block_order):
    rows, width = queries.shape

    def flip(x, axis):
        return lax.ppermute(x, axis, [(0, 1), (1, 0)])

    def shift(x, axis, by):
        size = lax.axis_size(axis)
        return lax.ppermute(x, axis, [(i, (i + by) % size) for i in range(size)])

    tile = lax.axis_index(T).astype(jnp.int32).reshape(1)
    place = jnp.stack([lax.axis_index(R), lax.axis_index(C)]).astype(jnp.int32)

    def over_tile(x):
        other = flip(x, "yh")
        return x, flip(x, "core"), other, flip(other, "core")

    part, us = project(tile, dec_grad, upstream, w_dec, over_tile(w_out))
    us = [us[0]] + [
        lax.ppermute(us[i], T, [(t, t ^ i) for t in range(4)]) for i in range(1, 4)
    ]
    part = lax.all_to_all(part.reshape(4 * SIDE, 32, width), T + (C,), 0, 0, tiled=True)

    hi = lax.reduce_precision(log_norm, 8, 7)
    mid = lax.reduce_precision(log_norm - hi, 8, 7)
    low = log_norm - hi - mid
    dest = block_order.reshape(-1, 1) * BLK + jnp.arange(BLK, dtype=jnp.int32)
    misc = [a.astype(bf16).reshape(-1, 128) for a in (hi, mid, low, dest)]
    misc = jnp.concatenate(misc + [jnp.zeros((2, 128), bf16)], 0)

    pay = pack(part.reshape(4, rows, width), queries, attn_out, misc, us)
    keys, values, pay = lax.optimization_barrier((keys, values, pay))
    ring = [jnp.concatenate([keys, values], 1)]
    for by, count in ((1, 4), (-1, 3)):
        moved = ring[0]
        for _ in range(count):
            moved = shift(moved, C, by)
            ring.append(moved)
    pay = lax.all_to_all(pay, R, 0, 0, tiled=True)
    dq, vk = attention(place, pay, ring)
    vk = lax.all_to_all(vk, C, 0, 0, tiled=True)
    dq = [dq[0]] + [
        lax.ppermute(dq[s], R, [(i, i ^ s) for i in range(SIDE)]) for s in range(1, SIDE)
    ]
    return tuple(finish_call(vk, *dq))


def solution(mesh):
    grid = Mesh(mesh.devices.reshape(2, 4, 8, 2, 2), S + T)
    return jax.shard_map(
        body,
        mesh=grid,
        in_specs=(
            P(S, T), P(S, T), P(S, T), P(S, T), P(T, S),
            P(S, T), P(S, T), P(None, T), P(T, None), P(S, None),
        ),
        out_specs=(P(S, T), P(S, T), P(S, T)),
        check_vma=False,
    )
```

time: 1160 us -> 137 us (0.12)
  waiting for transfers between devices: 715 us -> 50.2 us
  blocking collectives: 297 us -> 0 us
  matrix products: 87.4 us -> 0 us
  starting transfers between devices: 10.8 us -> 49.7 us
  Pallas kernels: 0 us -> 29.1 us
  local copies, waits for them, and re-layouts: 22 us -> 5.24 us
  between operations: 15.8 us -> 0.8 us
    all_gather x4 -> x0, waiting for transfers between devices: 671 us -> none  [the longest x1 276 us: body(): query_blk = lax.all_gather(queries, 'seq', axis=0, tiled=True)]
    all_gather x3 -> x0, blocking collectives: 297 us -> none  [the longest x1 151 us: body(): lax.all_gather(row_delta.T, 'seq', axis=0, tiled=True)]
    dot_general x8 -> x0, matrix products: 87.4 us -> none  [the longest x1 18 us: query_terms(): jnp.einsum('hqk,khd->qhd', d_scores, key_blk, preferred_element_type=jnp....]
    reduce_scatter x1 -> x0, waiting for transfers between devices: 33.7 us -> none  [body(): lax.psum_scatter(partial_rows, 'tile', scatter_dimension=1, tiled=True)]
    ppermute x0 -> x20, waiting for transfers between devices: none -> 32.6 us  [the longest x7 14.7 us: shift(): return lax.ppermute(x, axis, [(i, (i + by) % size) for i in range(size)])]
    ppermute x0 -> x20, starting transfers between devices: none -> 29.6 us  [the longest x7 12.9 us: body(): lax.ppermute(dq[s], R, [(i, i ^ s) for i in range(SIDE)])]
    pallas_call x0 -> x4, Pallas kernels: none -> 29.1 us  [the longest x1 23.4 us: attention(): pl.pallas_call(attention_kernel, in_specs=[pl.BlockSpec(memory_space=pltp...]
    all_gather x2 -> x0, local copies, waits for them, and re-layouts: 12.8 us -> none  [the longest x1 6.44 us: body(): key_blk = lax.all_gather(keys, 'seq', axis=0, tiled=True)]
  transfers between devices with their start and end apart: 6 -> 23, of which waited for: 5 -> 13; matrix products, arithmetic and copies ran while one was open for 7% -> 0% of each run, Pallas kernels for 0% -> 0%
where the time goes in v1:
time: 137 us; the launch traced here: 135 us
  waiting for transfers between devices  50.2 us (37%)
  starting transfers between devices  49.7 us (36%)
  Pallas kernels  29.1 us (21%)
  local copies, waits for them, and re-layouts  5.24 us (4%)
    pallas_call x1, Pallas kernels, attention(): pl.pallas_call(attention_kernel, in_specs=[pl.BlockSpec(memory_space=pltp...  23.4 us
    ppermute x7, waiting for transfers between devices, shift(): return lax.ppermute(x, axis, [(i, (i + by) % size) for i in range(size)])  14.7 us
    ppermute x7, starting transfers between devices, body(): lax.ppermute(dq[s], R, [(i, i ^ s) for i in range(SIDE)])  12.9 us
    all_to_all x1, waiting for transfers between devices, body(): vk = lax.all_to_all(vk, C, 0, 0, tiled=True)  12.9 us
    all_to_all x1, starting transfers between devices, body(): lax.all_to_all(part.reshape(4 * SIDE, 32, width), T + (C,), 0, 0, tiled=T...  11.5 us
    ppermute x7, starting transfers between devices, shift(): return lax.ppermute(x, axis, [(i, (i + by) % size) for i in range(size)])  9.79 us
    ppermute x3, waiting for transfers between devices, flip(): return lax.ppermute(x, axis, [(0, 1), (1, 0)])  8.08 us
    ppermute x3, waiting for transfers between devices, body(): lax.ppermute(us[i], T, [(t, t ^ i) for t in range(4)])  7.14 us
  transfers between devices with their start and end apart: 23, of which 13 were waited for; matrix products, arithmetic and copies ran while one was open for 0% of the time, Pallas kernels for 0%

profile of v1, /device:TPU:2, one launch (start us, length us, event | category | flops | bytes accessed | tf_op | source)
XLA Modules:
  0.0 135.1 jit_solution(9510735210245681743)
XLA Ops:
  0.6 0.0 copy-start.13
  0.7 3.3 %collective-permute-start.1 = (bf16[128,1024]{1,0:T(8,128)(2,1)}, bf16[128,1024]{1,0:T(8,128)(2,1)S(1)}, u32[]{:S(2)}, u32[]{:S(2)}) collective-permute-start(bf16[128,1024]{1,0:T(8,128)(2,1)} %refs_3_.1), channel_id=1, source_target_pairs={{0,2},{2,0},{1,3},{3,1},{4,6},{6,4},{5,7},{7,5},{8,10},{10,8},{9,1... | collective-permute-start | bytes 786440 | tf_op jit(solution)/shard_map/ppermute | solution.py:232
  4.0 0.0 collective-permute-start
  4.0 6.6 %collective-permute-done.1.refs_5_ = bf16[128,1024]{1,0:T(8,128)(2,1)S(1)} collective-permute-done((bf16[128,1024]{1,0:T(8,128)(2,1)}, bf16[128,1024]{1,0:T(8,128)(2,1)S(1)}, u32[]{:S(2)}, u32[]{:S(2)}) %collective-permute-start.1) | collective-permute-done | bytes 262176 | tf_op jit(solution)/shard_map/ppermute | solution.py:232
  10.5 0.0 collective-permute-start.2
  10.5 0.0 collective-permute-done.refs_4_
  10.5 1.5 %collective-permute-done.2.refs_6_ = bf16[128,1024]{1,0:T(8,128)(2,1)S(1)} collective-permute-done((bf16[128,1024]{1,0:T(8,128)(2,1)S(1)}, bf16[128,1024]{1,0:T(8,128)(2,1)S(1)}, u32[]{:S(2)}, u32[]{:S(2)}) %collective-permute-start.2) | collective-permute-done | bytes 262176 | tf_op jit(solution)/shard_map/ppermute | solution.py:232
  12.1 0.7 copy-done.9
  12.8 3.1 %project.1 = (bf16[4,256,128]{2,1,0:T(8,128)(2,1)}, bf16[256,128]{1,0:T(8,128)(2,1)}, bf16[256,128]{1,0:T(8,128)(2,1)}, bf16[256,128]{1,0:T(8,128)(2,1)}, bf16[256,128]{1,0:T(8,128)(2,1)}) custom-call(s32[1]{0:T(128)} %bitcast.2.tile_ref, bf16[256,256]{1,0:T(8,128)(2,1)} %refs_0_.1, bf16[256,256]{1,0:T(8,128)(2,1)} %refs_1_.1, bf16[1024,256]{1,0:T(8,128)(2,1)} %refs_2_.1, ...), custom_call_target="tpu_custom_call" | custom-call | tf_op jit(solution)/shard_map/project/pallas_call | solution.py:62
  15.9 11.5 %all-to-all-start = ((bf16[32,32,128]{2,1,0:T(8,128)(2,1)}), bf16[32,32,128]{2,1,0:T(8,128)(2,1)S(1)}, u32[]{:S(2)}, u32[]{:S(2)}) async-start(bf16[32,32,128]{2,1,0:T(8,128)(2,1)} %bitcast.22), calls=%async_computation | async-start | bytes 524288 | tf_op jit(solution)/shard_map/all_to_all | solution.py:249
  27.4 0.1 mul.24
  27.5 0.1 add.31
  27.6 0.1 add.28
  27.7 0.1 add.29
  27.8 0.4 collective-permute-start.3
  28.2 3.2 %collective-permute-start.4 = (bf16[256,128]{1,0:T(8,128)(2,1)}, bf16[256,128]{1,0:T(8,128)(2,1)S(1)}, u32[]{:S(2)}, u32[]{:S(2)}) collective-permute-start(bf16[256,128]{1,0:T(8,128)(2,1)} %get-tuple-element.16), channel_id=1, source_target_pairs={{0,2},{1,3},{2,0},{3,1},{4,6},{5,7},{6,4},{7,5},{8,10},{9,11},{10,... | collective-permute-start | bytes 196616 | tf_op jit(solution)/shard_map/ppermute | solution.py:247
  31.4 0.0 collective-permute-start.5
  31.5 0.1 concatenate.6.misc_ref
  31.5 0.0 collective-permute-done.3.u1_ref
  31.5 3.7 %collective-permute-done.4.u2_ref = bf16[256,128]{1,0:T(8,128)(2,1)S(1)} collective-permute-done((bf16[256,128]{1,0:T(8,128)(2,1)}, bf16[256,128]{1,0:T(8,128)(2,1)S(1)}, u32[]{:S(2)}, u32[]{:S(2)}) %collective-permute-start.4) | collective-permute-done | bytes 65568 | tf_op jit(solution)/shard_map/ppermute | solution.py:247
  35.2 3.4 %collective-permute-done.5.u3_ref = bf16[256,128]{1,0:T(8,128)(2,1)S(1)} collective-permute-done((bf16[256,128]{1,0:T(8,128)(2,1)}, bf16[256,128]{1,0:T(8,128)(2,1)S(1)}, u32[]{:S(2)}, u32[]{:S(2)}) %collective-permute-start.5) | collective-permute-done | bytes 65568 | tf_op jit(solution)/shard_map/ppermute | solution.py:247
  38.7 1.1 all-to-all-done
  39.8 0.0 copy-done
  39.8 0.8 copy-done.2
  40.6 1.7 %pack.1 = bf16[8,1040,128]{2,1,0:T(8,128)(2,1)} custom-call(bf16[4,256,128]{2,1,0:T(8,128)(2,1)S(1)} %bitcast.21, bf16[256,128]{1,0:T(8,128)(2,1)S(1)} %copy-done, bf16[256,128]{1,0:T(8,128)(2,1)S(1)} %copy-done.1, bf16[16,128]{1,0:T(8,128)(2,1)S(1)} %concatenate.6.misc_ref, bf16[256,128]{1,0:T(8,128)(2,1)S(1)} %copy-done.2, ...), custom_call_target="tpu_custom_call" | custom-call | tf_op jit(solution)/shard_map/pack/pallas_call | solution.py:98
  42.3 5.1 %all-to-all-start.1 = ((bf16[8,1040,128]{2,1,0:T(8,128)(2,1)}), bf16[8,1040,128]{2,1,0:T(8,128)(2,1)S(1)}, u32[]{:S(2)}, u32[]{:S(2)}) async-start(bf16[8,1040,128]{2,1,0:T(8,128)(2,1)} %pack.1), calls=%async_computation.1 | async-start | bytes 4259840 | tf_op jit(solution)/shard_map/all_to_all | solution.py:266
  47.5 2.5 %collective-permute-start.6 = (bf16[256,256]{1,0:T(8,128)(2,1)S(1)}, bf16[256,256]{1,0:T(8,128)(2,1)S(1)}, u32[]{:S(2)}, u32[]{:S(2)}) collective-permute-start(bf16[256,256]{1,0:T(8,128)(2,1)S(1)} %constant_dynamic-update-slice_fusion.refs_0_), channel_id=1, source_target_pairs={{0,4},{4,8},{8,12},{12,16},{16,20},{20,24},{24,28},{28,0},{1,5},{5... | collective-permute-start | bytes 393224 | tf_op jit(solution)/shard_map/ppermute | solution.py:236
  50.0 0.8 collective-permute-start.10
  50.8 3.3 %collective-permute-done.6.refs_1_ = bf16[256,256]{1,0:T(8,128)(2,1)S(1)} collective-permute-done((bf16[256,256]{1,0:T(8,128)(2,1)S(1)}, bf16[256,256]{1,0:T(8,128)(2,1)S(1)}, u32[]{:S(2)}, u32[]{:S(2)}) %collective-permute-start.6) | collective-permute-done | bytes 131104 | tf_op jit(solution)/shard_map/ppermute | solution.py:236
  54.1 0.8 collective-permute-start.7
  54.9 0.0 collective-permute-done.10.refs_5_
  54.9 2.4 %collective-permute-start.11 = (bf16[256,256]{1,0:T(8,128)(2,1)S(1)}, bf16[256,256]{1,0:T(8,128)(2,1)S(1)}, u32[]{:S(2)}, u32[]{:S(2)}) collective-permute-start(bf16[256,256]{1,0:T(8,128)(2,1)S(1)} %collective-permute-done.10.refs_5_), channel_id=1, source_target_pairs={{0,28},{4,0},{8,4},{12,8},{16,12},{20,16},{24,20},{28,24},{1,29},{... | collective-permute-start | bytes 393224 | tf_op jit(solution)/shard_map/ppermute | solution.py:236
  57.4 2.9 %collective-permute-done.7.refs_2_ = bf16[256,256]{1,0:T(8,128)(2,1)S(1)} collective-permute-done((bf16[256,256]{1,0:T(8,128)(2,1)S(1)}, bf16[256,256]{1,0:T(8,128)(2,1)S(1)}, u32[]{:S(2)}, u32[]{:S(2)}) %collective-permute-start.7) | collective-permute-done | bytes 131104 | tf_op jit(solution)/shard_map/ppermute | solution.py:236
  60.3 0.0 collective-permute-start.8
  60.3 0.0 collective-permute-done.11.refs_6_
  60.3 3.2 %collective-permute-start.12 = (bf16[256,256]{1,0:T(8,128)(2,1)S(1)}, bf16[256,256]{1,0:T(8,128)(2,1)S(1)}, u32[]{:S(2)}, u32[]{:S(2)}) collective-permute-start(bf16[256,256]{1,0:T(8,128)(2,1)S(1)} %collective-permute-done.11.refs_6_), channel_id=1, source_target_pairs={{0,28},{4,0},{8,4},{12,8},{16,12},{20,16},{24,20},{28,24},{1,29},{... | collective-permute-start | bytes 393224 | tf_op jit(solution)/shard_map/ppermute | solution.py:236
  63.5 2.9 %collective-permute-done.8.refs_3_ = bf16[256,256]{1,0:T(8,128)(2,1)S(1)} collective-permute-done((bf16[256,256]{1,0:T(8,128)(2,1)S(1)}, bf16[256,256]{1,0:T(8,128)(2,1)S(1)}, u32[]{:S(2)}, u32[]{:S(2)}) %collective-permute-start.8) | collective-permute-done | bytes 131104 | tf_op jit(solution)/shard_map/ppermute | solution.py:236
  66.5 0.0 collective-permute-start.9
  66.5 0.1 pad_add_fusion.place_ref
  66.6 0.0 collective-permute-done.12.refs_7_
  66.6 0.7 copy-done.3
  67.2 5.4 %collective-permute-done.9.refs_4_ = bf16[256,256]{1,0:T(8,128)(2,1)S(1)} collective-permute-done((bf16[256,256]{1,0:T(8,128)(2,1)S(1)}, bf16[256,256]{1,0:T(8,128)(2,1)S(1)}, u32[]{:S(2)}, u32[]{:S(2)}) %collective-permute-start.9) | collective-permute-done | bytes 131104 | tf_op jit(solution)/shard_map/ppermute | solution.py:236
  72.7 0.7 copy-done.5
  73.3 3.6 %all-to-all-done.1.pay_ref = bf16[8,1040,128]{2,1,0:T(8,128)(2,1)S(1)} async-done(((bf16[8,1040,128]{2,1,0:T(8,128)(2,1)}), bf16[8,1040,128]{2,1,0:T(8,128)(2,1)S(1)}, u32[]{:S(2)}, u32[]{:S(2)}) %all-to-all-start.1) | async-done | bytes 2129952 | tf_op jit(solution)/shard_map/all_to_all | solution.py:266
  76.9 0.9 copy-done.4
  77.8 0.9 copy-done.6
  78.7 23.4 %attention.1 = (bf16[8,128,256]{2,1,0:T(8,128)(2,1)S(1)}, bf16[8,2,256,128]{3,2,1,0:T(8,128)(2,1)}) custom-call(s32[2]{0:T(128)S(1)} %pad_add_fusion.place_ref, bf16[8,1040,128]{2,1,0:T(8,128)(2,1)S(1)} %all-to-all-done.1.pay_ref, bf16[256,256]{1,0:T(8,128)(2,1)S(1)} %constant_dynamic-update-slice_fusion.refs_0_, ...), custom_call_target="tpu_custom_call" | custom-call | flops 21474836480 | bytes 8388608 | tf_op jit(solution)/shard_map/attention/pallas_call | solution.py:191
  102.1 3.6 %all-to-all-start.2 = ((bf16[8,2,256,128]{3,2,1,0:T(8,128)(2,1)}), bf16[8,2,256,128]{3,2,1,0:T(8,128)(2,1)S(1)}, u32[]{:S(2)}, u32[]{:S(2)}) async-start(bf16[8,2,256,128]{3,2,1,0:T(8,128)(2,1)} %get-tuple-element.21), calls=%async_computation.2 | async-start | bytes 2097152 | tf_op jit(solution)/shard_map/all_to_all | solution.py:268
  105.8 0.1 collective-permute-start.19
  105.9 4.9 %collective-permute-start.18 = (bf16[128,256]{1,0:T(8,128)(2,1)S(1)}, bf16[128,256]{1,0:T(8,128)(2,1)S(1)}, u32[]{:S(2)}, u32[]{:S(2)}) collective-permute-start(bf16[128,256]{1,0:T(8,128)(2,1)S(1)} %get-tuple-element.24), channel_id=1, source_target_pairs={{0,192},{32,224},{64,128},{96,160},{128,64},{160,96},{192,0},{224,... | collective-permute-start | bytes 196616 | tf_op jit(solution)/shard_map/ppermute | solution.py:270
  110.8 1.1 collective-permute-start.17
  111.9 1.5 %collective-permute-start.16 = (bf16[128,256]{1,0:T(8,128)(2,1)S(1)}, bf16[128,256]{1,0:T(8,128)(2,1)S(1)}, u32[]{:S(2)}, u32[]{:S(2)}) collective-permute-start(bf16[128,256]{1,0:T(8,128)(2,1)S(1)} %get-tuple-element.26), channel_id=1, source_target_pairs={{0,128},{32,160},{64,192},{96,224},{128,0},{160,32},{192,64},{224,... | collective-permute-start | bytes 196616 | tf_op jit(solution)/shard_map/ppermute | solution.py:270
  113.3 1.5 %collective-permute-start.15 = (bf16[128,256]{1,0:T(8,128)(2,1)S(1)}, bf16[128,256]{1,0:T(8,128)(2,1)S(1)}, u32[]{:S(2)}, u32[]{:S(2)}) collective-permute-start(bf16[128,256]{1,0:T(8,128)(2,1)S(1)} %get-tuple-element.27), channel_id=1, source_target_pairs={{0,96},{32,64},{64,32},{96,0},{128,224},{160,192},{192,160},{224,1... | collective-permute-start | bytes 196616 | tf_op jit(solution)/shard_map/ppermute | solution.py:270
  114.8 0.0 collective-permute-done.19.refs_7_
  114.8 2.3 %collective-permute-start.14 = (bf16[128,256]{1,0:T(8,128)(2,1)S(1)}, bf16[128,256]{1,0:T(8,128)(2,1)S(1)}, u32[]{:S(2)}, u32[]{:S(2)}) collective-permute-start(bf16[128,256]{1,0:T(8,128)(2,1)S(1)} %get-tuple-element.28), channel_id=1, source_target_pairs={{0,64},{32,96},{64,0},{96,32},{128,192},{160,224},{192,128},{224,1... | collective-permute-start | bytes 196616 | tf_op jit(solution)/shard_map/ppermute | solution.py:270
  117.1 0.0 collective-permute-done.18.refs_6_
  117.1 1.6 %collective-permute-start.13 = (bf16[128,256]{1,0:T(8,128)(2,1)S(1)}, bf16[128,256]{1,0:T(8,128)(2,1)S(1)}, u32[]{:S(2)}, u32[]{:S(2)}) collective-permute-start(bf16[128,256]{1,0:T(8,128)(2,1)S(1)} %get-tuple-element.29), channel_id=1, source_target_pairs={{0,32},{32,0},{64,96},{96,64},{128,160},{160,128},{192,224},{224,1... | collective-permute-start | bytes 196616 | tf_op jit(solution)/shard_map/ppermute | solution.py:270
  118.7 0.0 collective-permute-done.17.refs_5_
  118.7 0.0 collective-permute-done.16.refs_4_
  118.7 0.0 collective-permute-done.15.refs_3_
  118.7 1.9 %collective-permute-done.14.refs_2_ = bf16[128,256]{1,0:T(8,128)(2,1)S(1)} collective-permute-done((bf16[128,256]{1,0:T(8,128)(2,1)S(1)}, bf16[128,256]{1,0:T(8,128)(2,1)S(1)}, u32[]{:S(2)}, u32[]{:S(2)}) %collective-permute-start.14) | collective-permute-done | bytes 65568 | tf_op jit(solution)/shard_map/ppermute | solution.py:270
  120.6 0.8 collective-permute-done.13.refs_1_
  121.4 12.9 %all-to-all-done.2.vk_ref = bf16[8,2,256,128]{3,2,1,0:T(8,128)(2,1)S(1)} async-done(((bf16[8,2,256,128]{3,2,1,0:T(8,128)(2,1)}), bf16[8,2,256,128]{3,2,1,0:T(8,128)(2,1)S(1)}, u32[]{:S(2)}, u32[]{:S(2)}) %all-to-all-start.2) | async-done | bytes 1048608 | tf_op jit(solution)/shard_map/all_to_all | solution.py:268
  134.2 0.9 finish.1
  (31 shorter events, 0.2 us)
Async XLA Ops:
  0.6 26.8 %copy-start.13 = (s32[1,64]{1,0:T(1,128)S(1)}, s32[1,64]{1,0:T(1,128)}, u32[]{:S(2)}) copy-start(s32[1,64]{1,0:T(1,128)} %param.19) | copy-start | bytes 772
  0.6 27.2 %copy-start.12 = (f32[2,256]{1,0:T(2,128)S(1)}, f32[2,256]{1,0:T(2,128)}, u32[]{:S(2)}) copy-start(f32[2,256]{1,0:T(2,128)} %param.14) | copy-start | bytes 6148
  0.7 39.1 %copy-start.1 = (bf16[256,128]{1,0:T(8,128)(2,1)S(1)}, bf16[256,128]{1,0:T(8,128)(2,1)}, u32[]{:S(2)}) copy-start(bf16[256,128]{1,0:T(8,128)(2,1)} %out_ref.1) | copy-start | bytes 196612
  0.7 39.1 %copy-start = (bf16[256,128]{1,0:T(8,128)(2,1)S(1)}, bf16[256,128]{1,0:T(8,128)(2,1)}, u32[]{:S(2)}) copy-start(bf16[256,128]{1,0:T(8,128)(2,1)} %q_ref.1) | copy-start | bytes 196612
  0.7 9.8 %collective-permute-start.1 = (bf16[128,1024]{1,0:T(8,128)(2,1)}, bf16[128,1024]{1,0:T(8,128)(2,1)S(1)}, u32[]{:S(2)}, u32[]{:S(2)}) collective-permute-start(bf16[128,1024]{1,0:T(8,128)(2,1)} %refs_3_.1), channel_id=1, source_target_pairs={{0,2},{2,0},{1,3},{3,1},{4,6},{6,4},{5,7},{7,5},{8,10},{10,8},{9,1... | collective-permute-start | bytes 786440 | tf_op jit(solution)/shard_map/ppermute | solution.py:232
  4.0 6.6 %collective-permute-start = (bf16[128,1024]{1,0:T(8,128)(2,1)}, bf16[128,1024]{1,0:T(8,128)(2,1)S(1)}, u32[]{:S(2)}, u32[]{:S(2)}) collective-permute-start(bf16[128,1024]{1,0:T(8,128)(2,1)} %refs_3_.1), channel_id=1, source_target_pairs={{0,1},{1,0},{2,3},{3,2},{4,5},{5,4},{6,7},{7,6},{8,9},{9,8},{10,11... | collective-permute-start | bytes 786440 | tf_op jit(solution)/shard_map/ppermute | solution.py:232
  10.5 1.5 %copy-start.7 = (bf16[128,1024]{1,0:T(8,128)(2,1)}, bf16[128,1024]{1,0:T(8,128)(2,1)S(1)}, u32[]{:S(2)}) copy-start(bf16[128,1024]{1,0:T(8,128)(2,1)S(1)} %collective-permute-done.1.refs_5_) | copy-start | bytes 786436
  10.5 1.5 %collective-permute-start.2 = (bf16[128,1024]{1,0:T(8,128)(2,1)S(1)}, bf16[128,1024]{1,0:T(8,128)(2,1)S(1)}, u32[]{:S(2)}, u32[]{:S(2)}) collective-permute-start(bf16[128,1024]{1,0:T(8,128)(2,1)S(1)} %collective-permute-done.1.refs_5_), channel_id=1, source_target_pairs={{0,1},{1,0},{2,3},{3,2},{4,5},{5,4},{6,7},{7,6},{8,9},{9,8},{10,11... | collective-permute-start | bytes 786440 | tf_op jit(solution)/shard_map/ppermute | solution.py:232
  10.5 1.5 %copy-start.8 = (bf16[128,1024]{1,0:T(8,128)(2,1)}, bf16[128,1024]{1,0:T(8,128)(2,1)S(1)}, u32[]{:S(2)}) copy-start(bf16[128,1024]{1,0:T(8,128)(2,1)S(1)} %collective-permute-done.refs_4_) | copy-start | bytes 786436
  12.1 0.7 copy-start.9
  15.9 23.9 %all-to-all-start = ((bf16[32,32,128]{2,1,0:T(8,128)(2,1)}), bf16[32,32,128]{2,1,0:T(8,128)(2,1)S(1)}, u32[]{:S(2)}, u32[]{:S(2)}) async-start(bf16[32,32,128]{2,1,0:T(8,128)(2,1)} %bitcast.22), calls=%async_computation | async-start | bytes 524288 | tf_op jit(solution)/shard_map/all_to_all | solution.py:249
  27.8 3.7 %collective-permute-start.3 = (bf16[256,128]{1,0:T(8,128)(2,1)}, bf16[256,128]{1,0:T(8,128)(2,1)S(1)}, u32[]{:S(2)}, u32[]{:S(2)}) collective-permute-start(bf16[256,128]{1,0:T(8,128)(2,1)} %get-tuple-element.15), channel_id=1, source_target_pairs={{0,1},{1,0},{2,3},{3,2},{4,5},{5,4},{6,7},{7,6},{8,9},{9,8},{10,11... | collective-permute-start | bytes 196616 | tf_op jit(solution)/shard_map/ppermute | solution.py:247
  28.2 7.1 %collective-permute-start.4 = (bf16[256,128]{1,0:T(8,128)(2,1)}, bf16[256,128]{1,0:T(8,128)(2,1)S(1)}, u32[]{:S(2)}, u32[]{:S(2)}) collective-permute-start(bf16[256,128]{1,0:T(8,128)(2,1)} %get-tuple-element.16), channel_id=1, source_target_pairs={{0,2},{1,3},{2,0},{3,1},{4,6},{5,7},{6,4},{7,5},{8,10},{9,11},{10,... | collective-permute-start | bytes 196616 | tf_op jit(solution)/shard_map/ppermute | solution.py:247
  31.4 7.3 %collective-permute-start.5 = (bf16[256,128]{1,0:T(8,128)(2,1)}, bf16[256,128]{1,0:T(8,128)(2,1)S(1)}, u32[]{:S(2)}, u32[]{:S(2)}) collective-permute-start(bf16[256,128]{1,0:T(8,128)(2,1)} %get-tuple-element.17), channel_id=1, source_target_pairs={{0,3},{1,2},{2,1},{3,0},{4,7},{5,6},{6,5},{7,4},{8,11},{9,10},{10,... | collective-permute-start | bytes 196616 | tf_op jit(solution)/shard_map/ppermute | solution.py:247
  39.8 0.8 copy-start.2
  42.3 5.1 %copy-start.10 = (bf16[256,128]{1,0:T(8,128)(2,1)S(1)}, bf16[256,128]{1,0:T(8,128)(2,1)}, u32[]{:S(2)}) copy-start(bf16[256,128]{1,0:T(8,128)(2,1)} %param.11) | copy-start | bytes 196612
  42.3 5.1 %copy-start.11 = (bf16[256,128]{1,0:T(8,128)(2,1)S(1)}, bf16[256,128]{1,0:T(8,128)(2,1)}, u32[]{:S(2)}) copy-start(bf16[256,128]{1,0:T(8,128)(2,1)} %param.12) | copy-start | bytes 196612
  42.3 34.6 %all-to-all-start.1 = ((bf16[8,1040,128]{2,1,0:T(8,128)(2,1)}), bf16[8,1040,128]{2,1,0:T(8,128)(2,1)S(1)}, u32[]{:S(2)}, u32[]{:S(2)}) async-start(bf16[8,1040,128]{2,1,0:T(8,128)(2,1)} %pack.1), calls=%async_computation.1 | async-start | bytes 4259840 | tf_op jit(solution)/shard_map/all_to_all | solution.py:266
  47.5 6.7 %collective-permute-start.6 = (bf16[256,256]{1,0:T(8,128)(2,1)S(1)}, bf16[256,256]{1,0:T(8,128)(2,1)S(1)}, u32[]{:S(2)}, u32[]{:S(2)}) collective-permute-start(bf16[256,256]{1,0:T(8,128)(2,1)S(1)} %constant_dynamic-update-slice_fusion.refs_0_), channel_id=1, source_target_pairs={{0,4},{4,8},{8,12},{12,16},{16,20},{20,24},{24,28},{28,0},{1,5},{5... | collective-permute-start | bytes 393224 | tf_op jit(solution)/shard_map/ppermute | solution.py:236
  50.0 5.0 %collective-permute-start.10 = (bf16[256,256]{1,0:T(8,128)(2,1)S(1)}, bf16[256,256]{1,0:T(8,128)(2,1)S(1)}, u32[]{:S(2)}, u32[]{:S(2)}) collective-permute-start(bf16[256,256]{1,0:T(8,128)(2,1)S(1)} %constant_dynamic-update-slice_fusion.refs_0_), channel_id=1, source_target_pairs={{0,28},{4,0},{8,4},{12,8},{16,12},{20,16},{24,20},{28,24},{1,29},{... | collective-permute-start | bytes 393224 | tf_op jit(solution)/shard_map/ppermute | solution.py:236
  54.1 6.2 %collective-permute-start.7 = (bf16[256,256]{1,0:T(8,128)(2,1)S(1)}, bf16[256,256]{1,0:T(8,128)(2,1)S(1)}, u32[]{:S(2)}, u32[]{:S(2)}) collective-permute-start(bf16[256,256]{1,0:T(8,128)(2,1)S(1)} %collective-permute-done.6.refs_1_), channel_id=1, source_target_pairs={{0,4},{4,8},{8,12},{12,16},{16,20},{20,24},{24,28},{28,0},{1,5},{5... | collective-permute-start | bytes 393224 | tf_op jit(solution)/shard_map/ppermute | solution.py:236
  54.9 5.4 %collective-permute-start.11 = (bf16[256,256]{1,0:T(8,128)(2,1)S(1)}, bf16[256,256]{1,0:T(8,128)(2,1)S(1)}, u32[]{:S(2)}, u32[]{:S(2)}) collective-permute-start(bf16[256,256]{1,0:T(8,128)(2,1)S(1)} %collective-permute-done.10.refs_5_), channel_id=1, source_target_pairs={{0,28},{4,0},{8,4},{12,8},{16,12},{20,16},{24,20},{28,24},{1,29},{... | collective-permute-start | bytes 393224 | tf_op jit(solution)/shard_map/ppermute | solution.py:236
  60.3 6.2 %collective-permute-start.8 = (bf16[256,256]{1,0:T(8,128)(2,1)S(1)}, bf16[256,256]{1,0:T(8,128)(2,1)S(1)}, u32[]{:S(2)}, u32[]{:S(2)}) collective-permute-start(bf16[256,256]{1,0:T(8,128)(2,1)S(1)} %collective-permute-done.7.refs_2_), channel_id=1, source_target_pairs={{0,4},{4,8},{8,12},{12,16},{16,20},{20,24},{24,28},{28,0},{1,5},{5... | collective-permute-start | bytes 393224 | tf_op jit(solution)/shard_map/ppermute | solution.py:236
  60.3 6.3 %collective-permute-start.12 = (bf16[256,256]{1,0:T(8,128)(2,1)S(1)}, bf16[256,256]{1,0:T(8,128)(2,1)S(1)}, u32[]{:S(2)}, u32[]{:S(2)}) collective-permute-start(bf16[256,256]{1,0:T(8,128)(2,1)S(1)} %collective-permute-done.11.refs_6_), channel_id=1, source_target_pairs={{0,28},{4,0},{8,4},{12,8},{16,12},{20,16},{24,20},{28,24},{1,29},{... | collective-permute-start | bytes 393224 | tf_op jit(solution)/shard_map/ppermute | solution.py:236
  66.5 6.2 %collective-permute-start.9 = (bf16[256,256]{1,0:T(8,128)(2,1)S(1)}, bf16[256,256]{1,0:T(8,128)(2,1)S(1)}, u32[]{:S(2)}, u32[]{:S(2)}) collective-permute-start(bf16[256,256]{1,0:T(8,128)(2,1)S(1)} %collective-permute-done.8.refs_3_), channel_id=1, source_target_pairs={{0,4},{4,8},{8,12},{12,16},{16,20},{20,24},{24,28},{28,0},{1,5},{5... | collective-permute-start | bytes 393224 | tf_op jit(solution)/shard_map/ppermute | solution.py:236
  66.6 0.7 copy-start.3
  72.7 0.7 copy-start.5
  76.9 0.9 copy-start.4
  77.8 0.9 copy-start.6
  102.1 32.1 %all-to-all-start.2 = ((bf16[8,2,256,128]{3,2,1,0:T(8,128)(2,1)}), bf16[8,2,256,128]{3,2,1,0:T(8,128)(2,1)S(1)}, u32[]{:S(2)}, u32[]{:S(2)}) async-start(bf16[8,2,256,128]{3,2,1,0:T(8,128)(2,1)} %get-tuple-element.21), calls=%async_computation.2 | async-start | bytes 2097152 | tf_op jit(solution)/shard_map/all_to_all | solution.py:268
  105.8 9.0 %collective-permute-start.19 = (bf16[128,256]{1,0:T(8,128)(2,1)S(1)}, bf16[128,256]{1,0:T(8,128)(2,1)S(1)}, u32[]{:S(2)}, u32[]{:S(2)}) collective-permute-start(bf16[128,256]{1,0:T(8,128)(2,1)S(1)} %get-tuple-element.23), channel_id=1, source_target_pairs={{0,224},{32,192},{64,160},{96,128},{128,96},{160,64},{192,32},{224... | collective-permute-start | bytes 196616 | tf_op jit(solution)/shard_map/ppermute | solution.py:270
  105.9 11.3 %collective-permute-start.18 = (bf16[128,256]{1,0:T(8,128)(2,1)S(1)}, bf16[128,256]{1,0:T(8,128)(2,1)S(1)}, u32[]{:S(2)}, u32[]{:S(2)}) collective-permute-start(bf16[128,256]{1,0:T(8,128)(2,1)S(1)} %get-tuple-element.24), channel_id=1, source_target_pairs={{0,192},{32,224},{64,128},{96,160},{128,64},{160,96},{192,0},{224,... | collective-permute-start | bytes 196616 | tf_op jit(solution)/shard_map/ppermute | solution.py:270
  110.8 7.9 %collective-permute-start.17 = (bf16[128,256]{1,0:T(8,128)(2,1)S(1)}, bf16[128,256]{1,0:T(8,128)(2,1)S(1)}, u32[]{:S(2)}, u32[]{:S(2)}) collective-permute-start(bf16[128,256]{1,0:T(8,128)(2,1)S(1)} %get-tuple-element.25), channel_id=1, source_target_pairs={{0,160},{32,128},{64,224},{96,192},{128,32},{160,0},{192,96},{224,... | collective-permute-start | bytes 196616 | tf_op jit(solution)/shard_map/ppermute | solution.py:270
  111.9 6.8 %collective-permute-start.16 = (bf16[128,256]{1,0:T(8,128)(2,1)S(1)}, bf16[128,256]{1,0:T(8,128)(2,1)S(1)}, u32[]{:S(2)}, u32[]{:S(2)}) collective-permute-start(bf16[128,256]{1,0:T(8,128)(2,1)S(1)} %get-tuple-element.26), channel_id=1, source_target_pairs={{0,128},{32,160},{64,192},{96,224},{128,0},{160,32},{192,64},{224,... | collective-permute-start | bytes 196616 | tf_op jit(solution)/shard_map/ppermute | solution.py:270
  113.3 5.4 %collective-permute-start.15 = (bf16[128,256]{1,0:T(8,128)(2,1)S(1)}, bf16[128,256]{1,0:T(8,128)(2,1)S(1)}, u32[]{:S(2)}, u32[]{:S(2)}) collective-permute-start(bf16[128,256]{1,0:T(8,128)(2,1)S(1)} %get-tuple-element.27), channel_id=1, source_target_pairs={{0,96},{32,64},{64,32},{96,0},{128,224},{160,192},{192,160},{224,1... | collective-permute-start | bytes 196616 | tf_op jit(solution)/shard_map/ppermute | solution.py:270
  114.8 5.8 %collective-permute-start.14 = (bf16[128,256]{1,0:T(8,128)(2,1)S(1)}, bf16[128,256]{1,0:T(8,128)(2,1)S(1)}, u32[]{:S(2)}, u32[]{:S(2)}) collective-permute-start(bf16[128,256]{1,0:T(8,128)(2,1)S(1)} %get-tuple-element.28), channel_id=1, source_target_pairs={{0,64},{32,96},{64,0},{96,32},{128,192},{160,224},{192,128},{224,1... | collective-permute-start | bytes 196616 | tf_op jit(solution)/shard_map/ppermute | solution.py:270
  117.1 4.3 %collective-permute-start.13 = (bf16[128,256]{1,0:T(8,128)(2,1)S(1)}, bf16[128,256]{1,0:T(8,128)(2,1)S(1)}, u32[]{:S(2)}, u32[]{:S(2)}) collective-permute-start(bf16[128,256]{1,0:T(8,128)(2,1)S(1)} %get-tuple-element.29), channel_id=1, source_target_pairs={{0,32},{32,0},{64,96},{96,64},{128,160},{160,128},{192,224},{224,1... | collective-permute-start | bytes 196616 | tf_op jit(solution)/shard_map/ppermute | solution.py:270

commit v2 on v1

--- a/solution.py
+++ b/solution.py
@@ -1,3 +1,5 @@
+import functools
+
 import jax
 import jax.numpy as jnp
 from jax import lax
@@ -10,7 +12,9 @@
 BLK = 4
 SIDE = 8
 PAIR = 2
-RING = (0, 1, 2, 3, 4, -1, -2, -3)
+HALF = 4
+FAR = (4, 3, -3, 2)
+NEAR = (-2, 1, -1, 0)
 VMEM = 24 << 20
 LARGE = 60 << 20
 R = ("yl", "x")
@@ -127,31 +131,38 @@
     return d_out, nt(head_rows, hi) + nt(head_rows, mid) + nt(head_rows, low)
 
 
-def attention_kernel(place_ref, pay_ref, *refs):
-    kv_refs = refs[:SIDE]
-    dq_ref, vk_ref, kt_ref, dv_acc, dk_acc = refs[SIDE:]
+def attention_kernel(far, pay_ref, *refs):
+    kv_refs, refs = refs[:HALF], refs[HALF:]
+    if far:
+        shared, vk_refs, (kt_ref, dv_acc, dk_acc) = refs[:3], refs[3 : 3 + HALF], refs[3 + HALF :]
+        dq_out = None
+    else:
+        shared, dq_out, refs = refs[:3], refs[3], refs[4:]
+        vk_refs, (kt_ref, dv_acc, dk_acc) = refs[:HALF], refs[HALF:]
     dv_acc[...] = jnp.zeros_like(dv_acc)
     dk_acc[...] = jnp.zeros_like(dk_acc)
-    for t in range(SIDE):
+    for t in range(HALF):
         kt_ref[:, t * 256 : (t + 1) * 256] = kv_refs[t][:, 0:128].astype(f32).T.astype(bf16)
 
     def step_of(step, carry):
-        attention_step(step, place_ref, pay_ref, kv_refs, kt_ref, dq_ref, dv_acc, dk_acc)
+        attention_step(step, pay_ref, kv_refs, shared, dq_out, kt_ref, dv_acc, dk_acc)
         return carry
 
     lax.fori_loop(0, SIDE // PAIR, step_of, 0)
-    for t in range(SIDE):
-        c = (place_ref[1] - RING[t]) & (SIDE - 1)
-        vk_ref[c, 0] = dv_acc[t * 256 : (t + 1) * 256, :].astype(bf16)
-        vk_ref[c, 1] = dk_acc[t * 256 : (t + 1) * 256, :].astype(bf16)
-
-
-def attention_step(step, place_ref, pay_ref, kv_refs, kt_ref, dq_ref, dv_acc, dk_acc):
+    for t in range(HALF):
+        vk_refs[t][0] = dv_acc[t * 256 : (t + 1) * 256, :].astype(bf16)
+        vk_refs[t][1] = dk_acc[t * 256 : (t + 1) * 256, :].astype(bf16)
+
+
+def attention_step(step, pay_ref, kv_refs, shared, dq_out, kt_ref, dv_acc, dk_acc):
+    d_out_ref, delta_ref, dq_ref = shared
     masks = head_masks()
     chains = []
     for i in range(PAIR):
         r = step * PAIR + i
-        d_out, delta = token_grads(pay_ref, r)
+        if dq_out is None:
+            d_out_ref[r], delta_ref[r] = token_grads(pay_ref, r)
+        d_out, delta = d_out_ref[r], delta_ref[r]
         query = pay_ref[r, 0:256] * bf16(0.125)
         misc = pay_ref[r, 1024:1040].astype(f32)
         parts = misc[0:4] + misc[4:8] + misc[8:12]
@@ -167,9 +178,9 @@
 
     dq = [jnp.zeros((HD, 256), f32) for _ in chains]
     later = scores_of(0)
-    for t in range(SIDE):
+    for t in range(HALF):
         now = later
-        if t + 1 < SIDE:
+        if t + 1 < HALF:
             later = scores_of(t + 1)
         keys = slice(t * 256, (t + 1) * 256)
         probs, d_scores = [], []
@@ -182,29 +193,42 @@
         dv_acc[keys, :] += nn(jnp.concatenate(probs, 1), grads)
         dk_acc[keys, :] += nn(jnp.concatenate(d_scores, 1), queries)
     for i in range(PAIR):
+        r = step * PAIR + i
         both = jnp.concatenate(dq[2 * i : 2 * i + 2], 0)
-        dq_ref[(step * PAIR + i) ^ place_ref[0]] = (both * 0.125).astype(bf16)
-
-
-def attention(place, pay, ring):
-    dq_shape, vk_shape = (SIDE, 128, 256), (SIDE, 2, 256, 128)
-    return pl.pallas_call(
-        attention_kernel,
-        in_specs=[pl.BlockSpec(memory_space=pltpu.SMEM)] + [pl.BlockSpec(memory_space=pltpu.VMEM)] * 9,
-        out_shape=[jax.ShapeDtypeStruct(dq_shape, bf16), jax.ShapeDtypeStruct(vk_shape, bf16)],
+        if dq_out is None:
+            dq_ref[r] = both
+        else:
+            dq_out[r] = ((dq_ref[r] + both) * 0.125).astype(bf16)
+
+
+SHARED = [
+    jax.ShapeDtypeStruct((SIDE, 256, 128), bf16),
+    jax.ShapeDtypeStruct((SIDE, 8, 256), f32),
+    jax.ShapeDtypeStruct((SIDE, 128, 256), f32),
+]
+
+
+def attention(pay, kv, shared=None):
+    far = shared is None
+    outs = SHARED if far else [jax.ShapeDtypeStruct((SIDE, 128, 256), bf16)]
+    ins = [pay, *kv] + ([] if far else list(shared))
+    out = pl.pallas_call(
+        functools.partial(attention_kernel, far),
+        out_shape=outs + [jax.ShapeDtypeStruct((2, 256, 128), bf16)] * HALF,
         scratch_shapes=[
-            pltpu.VMEM((128, SIDE * 256), bf16),
-            pltpu.VMEM((SIDE * 256, 128), f32),
-            pltpu.VMEM((SIDE * 256, 128), f32),
+            pltpu.VMEM((128, HALF * 256), bf16),
+            pltpu.VMEM((HALF * 256, 128), f32),
+            pltpu.VMEM((HALF * 256, 128), f32),
         ],
         compiler_params=pltpu.CompilerParams(vmem_limit_bytes=VMEM),
-        cost_estimate=pl.CostEstimate(flops=20 << 30, bytes_accessed=1 << 23, transcendentals=1 << 23),
-        name="attention",
-    )(place, pay, *ring)
-
-
-def finish_kernel(vk_ref, *refs):
-    dq_refs, (dq_ref, dk_ref, dv_ref) = refs[:SIDE], refs[SIDE:]
+        cost_estimate=pl.CostEstimate(flops=14 << 30, bytes_accessed=1 << 22, transcendentals=1 << 22),
+        name="far" if far else "near",
+    )(*ins)
+    return out[: len(outs)], out[len(outs) :]
+
+
+def finish_kernel(*refs):
+    vk_refs, (dq_parts, dq_ref, dk_ref, dv_ref) = refs[:SIDE], refs[SIDE:]
 
     def total(parts):
         out = parts[0].astype(f32)
@@ -212,9 +236,9 @@
             out += part.astype(f32)
         return out
 
-    dq_ref[...] = total([ref[...] for ref in dq_refs]).T.astype(bf16)
-    dv_ref[...] = total([vk_ref[i, 0] for i in range(SIDE)]).astype(bf16)
-    dk_ref[...] = total([vk_ref[i, 1] for i in range(SIDE)]).astype(bf16)
+    dq_ref[...] = total([dq_parts[i] for i in range(SIDE)]).T.astype(bf16)
+    dv_ref[...] = total([ref[0] for ref in vk_refs]).astype(bf16)
+    dk_ref[...] = total([ref[1] for ref in vk_refs]).astype(bf16)
 
 
 finish_call = pl.pallas_call(
@@ -236,7 +260,6 @@
         return lax.ppermute(x, axis, [(i, (i + by) % size) for i in range(size)])
 
     tile = lax.axis_index(T).astype(jnp.int32).reshape(1)
-    place = jnp.stack([lax.axis_index(R), lax.axis_index(C)]).astype(jnp.int32)
 
     def over_tile(x):
         other = flip(x, "yh")
@@ -257,19 +280,18 @@
 
     pay = pack(part.reshape(4, rows, width), queries, attn_out, misc, us)
     keys, values, pay = lax.optimization_barrier((keys, values, pay))
-    ring = [jnp.concatenate([keys, values], 1)]
+    ring = {0: jnp.concatenate([keys, values], 1)}
     for by, count in ((1, 4), (-1, 3)):
-        moved = ring[0]
-        for _ in range(count):
-            moved = shift(moved, C, by)
-            ring.append(moved)
+        for hop in range(1, count + 1):
+            ring[by * hop] = shift(ring[by * (hop - 1)], C, by)
     pay = lax.all_to_all(pay, R, 0, 0, tiled=True)
-    dq, vk = attention(place, pay, ring)
-    vk = lax.all_to_all(vk, C, 0, 0, tiled=True)
-    dq = [dq[0]] + [
-        lax.ppermute(dq[s], R, [(i, i ^ s) for i in range(SIDE)]) for s in range(1, SIDE)
-    ]
-    return tuple(finish_call(vk, *dq))
+    shared, vk_far = attention(pay, [ring[s] for s in FAR])
+    vk_far = [shift(vk, C, -s) for s, vk in zip(FAR, vk_far)]
+    (dq,), vk_near = attention(pay, [ring[s] for s in NEAR], shared)
+    vk_near = [shift(vk, C, -s) if s else vk for s, vk in zip(NEAR, vk_near)]
+    vk_far, dq = lax.optimization_barrier((vk_far, dq))
+    dq = lax.all_to_all(dq, R, 0, 0, tiled=True)
+    return tuple(finish_call(*vk_far, *vk_near, dq))
 
 
 def solution(mesh):

time: 137 us -> 131 us (0.956); the launches traced: 135 us -> 131 us
  waiting for transfers between devices: 50.2 us -> 41.9 us
  starting transfers between devices: 49.7 us -> 55.5 us
  local copies, waits for them, and re-layouts: 5.24 us -> 3.38 us
    ppermute x7 -> x14, starting transfers between devices: 9.79 us -> 24.8 us  [shift(): return lax.ppermute(x, axis, [(i, (i + by) % size) for i in range(size)])]
    ppermute x7 -> x0, starting transfers between devices: 12.9 us -> none  [body(): lax.ppermute(dq[s], R, [(i, i ^ s) for i in range(SIDE)])]
    all_to_all x1, waiting for transfers between devices: 12.9 us -> 0.01 us  [body(): dq = lax.all_to_all(dq, R, 0, 0, tiled=True)]
    ppermute x7 -> x14, waiting for transfers between devices: 14.7 us -> 21.3 us  [shift(): return lax.ppermute(x, axis, [(i, (i + by) % size) for i in range(size)])]
    all_to_all x1, starting transfers between devices: 3.56 us -> 7.29 us  [body(): dq = lax.all_to_all(dq, R, 0, 0, tiled=True)]
    ppermute x7 -> x0, waiting for transfers between devices: 2.69 us -> none  [body(): lax.ppermute(dq[s], R, [(i, i ^ s) for i in range(SIDE)])]
    unnamed x29 -> x25, local copies, waits for them, and re-layouts: 4.7 us -> 2.87 us
    pallas_call x2 -> x3, Pallas kernels: 24.3 us -> 24.3 us  [the longest x2 23.4 us: attention(): pl.pallas_call(functools.partial(attention_kernel, far), out_shape=outs +...]
  transfers between devices with their start and end apart: 23 -> 23, of which waited for: 13 -> 12; matrix products, arithmetic and copies ran while one was open for 0% -> 0% of each run, Pallas kernels for 0% -> 9%
where the time goes in v2:
time: 131 us
  starting transfers between devices  55.5 us (42%)
  waiting for transfers between devices  41.9 us (32%)
  Pallas kernels  29.1 us (22%)
  local copies, waits for them, and re-layouts  3.38 us (3%)
    ppermute x14, starting transfers between devices, shift(): return lax.ppermute(x, axis, [(i, (i + by) % size) for i in range(size)])  24.8 us
    pallas_call x2, Pallas kernels, attention(): pl.pallas_call(functools.partial(attention_kernel, far), out_shape=outs +...  23.4 us
    ppermute x14, waiting for transfers between devices, shift(): return lax.ppermute(x, axis, [(i, (i + by) % size) for i in range(size)])  21.3 us
    all_to_all x1, starting transfers between devices, body(): lax.all_to_all(part.reshape(4 * SIDE, 32, width), T + (C,), 0, 0, tiled=T...  11.5 us
    ppermute x3, waiting for transfers between devices, flip(): return lax.ppermute(x, axis, [(0, 1), (1, 0)])  8.08 us
    all_to_all x1, starting transfers between devices, body(): dq = lax.all_to_all(dq, R, 0, 0, tiled=True)  7.29 us
    ppermute x3, waiting for transfers between devices, body(): lax.ppermute(us[i], T, [(t, t ^ i) for t in range(4)])  7.14 us
    all_to_all x1, starting transfers between devices, body(): pay = lax.all_to_all(pay, R, 0, 0, tiled=True)  5.07 us
  transfers between devices with their start and end apart: 23, of which 12 were waited for; matrix products, arithmetic and copies ran while one was open for 0% of the time, Pallas kernels for 9%

profile of v2, /device:TPU:2, one launch (start us, length us, event | category | flops | bytes accessed | tf_op | source)
XLA Modules:
  0.0 130.7 jit_solution(10563418549116590152)
XLA Ops:
  0.6 0.0 copy-start.11
  0.7 3.3 %collective-permute-start.1 = (bf16[128,1024]{1,0:T(8,128)(2,1)}, bf16[128,1024]{1,0:T(8,128)(2,1)S(1)}, u32[]{:S(2)}, u32[]{:S(2)}) collective-permute-start(bf16[128,1024]{1,0:T(8,128)(2,1)} %refs_3_.1), channel_id=1, source_target_pairs={{0,2},{2,0},{1,3},{3,1},{4,6},{6,4},{5,7},{7,5},{8,10},{10,8},{9,1... | collective-permute-start | bytes 786440 | tf_op jit(solution)/shard_map/ppermute | solution.py:256
  4.0 0.0 collective-permute-start
  4.0 6.6 %collective-permute-done.1.refs_5_ = bf16[128,1024]{1,0:T(8,128)(2,1)S(1)} collective-permute-done((bf16[128,1024]{1,0:T(8,128)(2,1)}, bf16[128,1024]{1,0:T(8,128)(2,1)S(1)}, u32[]{:S(2)}, u32[]{:S(2)}) %collective-permute-start.1) | collective-permute-done | bytes 262176 | tf_op jit(solution)/shard_map/ppermute | solution.py:256
  10.5 0.0 collective-permute-start.2
  10.5 0.0 collective-permute-done.refs_4_
  10.5 1.5 %collective-permute-done.2.refs_6_ = bf16[128,1024]{1,0:T(8,128)(2,1)S(1)} collective-permute-done((bf16[128,1024]{1,0:T(8,128)(2,1)S(1)}, bf16[128,1024]{1,0:T(8,128)(2,1)S(1)}, u32[]{:S(2)}, u32[]{:S(2)}) %collective-permute-start.2) | collective-permute-done | bytes 262176 | tf_op jit(solution)/shard_map/ppermute | solution.py:256
  12.1 0.0 copy-done.6
  12.1 0.7 copy-done.7
  12.8 3.1 %project.1 = (bf16[4,256,128]{2,1,0:T(8,128)(2,1)}, bf16[256,128]{1,0:T(8,128)(2,1)}, bf16[256,128]{1,0:T(8,128)(2,1)}, bf16[256,128]{1,0:T(8,128)(2,1)}, bf16[256,128]{1,0:T(8,128)(2,1)}) custom-call(s32[1]{0:T(128)} %bitcast.tile_ref, bf16[256,256]{1,0:T(8,128)(2,1)} %refs_0_.1, bf16[256,256]{1,0:T(8,128)(2,1)} %refs_1_.1, bf16[1024,256]{1,0:T(8,128)(2,1)} %refs_2_.1, ...), custom_call_target="tpu_custom_call" | custom-call | tf_op jit(solution)/shard_map/project/pallas_call | solution.py:66
  15.9 11.5 %all-to-all-start = ((bf16[32,32,128]{2,1,0:T(8,128)(2,1)}), bf16[32,32,128]{2,1,0:T(8,128)(2,1)S(1)}, u32[]{:S(2)}, u32[]{:S(2)}) async-start(bf16[32,32,128]{2,1,0:T(8,128)(2,1)} %bitcast.4), calls=%async_computation | async-start | bytes 524288 | tf_op jit(solution)/shard_map/all_to_all | solution.py:272
  27.4 0.0 copy-done.11
  27.4 0.1 mul.20
  27.5 0.1 add.24
  27.6 0.1 add.25
  27.7 0.1 add.27
  27.8 0.4 collective-permute-start.3
  28.2 3.2 %collective-permute-start.4 = (bf16[256,128]{1,0:T(8,128)(2,1)}, bf16[256,128]{1,0:T(8,128)(2,1)S(1)}, u32[]{:S(2)}, u32[]{:S(2)}) collective-permute-start(bf16[256,128]{1,0:T(8,128)(2,1)} %get-tuple-element.31), channel_id=1, source_target_pairs={{0,2},{1,3},{2,0},{3,1},{4,6},{5,7},{6,4},{7,5},{8,10},{9,11},{10,... | collective-permute-start | bytes 196616 | tf_op jit(solution)/shard_map/ppermute | solution.py:270
  31.4 0.0 collective-permute-start.5
  31.4 0.1 concatenate.6.misc_ref
  31.5 0.0 collective-permute-done.3.u1_ref
  31.5 3.7 %collective-permute-done.4.u2_ref = bf16[256,128]{1,0:T(8,128)(2,1)S(1)} collective-permute-done((bf16[256,128]{1,0:T(8,128)(2,1)}, bf16[256,128]{1,0:T(8,128)(2,1)S(1)}, u32[]{:S(2)}, u32[]{:S(2)}) %collective-permute-start.4) | collective-permute-done | bytes 65568 | tf_op jit(solution)/shard_map/ppermute | solution.py:270
  35.2 3.4 %collective-permute-done.5.u3_ref = bf16[256,128]{1,0:T(8,128)(2,1)S(1)} collective-permute-done((bf16[256,128]{1,0:T(8,128)(2,1)}, bf16[256,128]{1,0:T(8,128)(2,1)S(1)}, u32[]{:S(2)}, u32[]{:S(2)}) %collective-permute-start.5) | collective-permute-done | bytes 65568 | tf_op jit(solution)/shard_map/ppermute | solution.py:270
  38.6 1.1 all-to-all-done
  39.8 0.0 copy-done
  39.8 0.8 copy-done.2
  40.6 1.7 %pack.1 = bf16[8,1040,128]{2,1,0:T(8,128)(2,1)} custom-call(bf16[4,256,128]{2,1,0:T(8,128)(2,1)S(1)} %bitcast.3, bf16[256,128]{1,0:T(8,128)(2,1)S(1)} %copy-done, bf16[256,128]{1,0:T(8,128)(2,1)S(1)} %copy-done.1, bf16[16,128]{1,0:T(8,128)(2,1)S(1)} %concatenate.6.misc_ref, bf16[256,128]{1,0:T(8,128)(2,1)S(1)} %copy-done.2, ...), custom_call_target="tpu_custom_call" | custom-call | tf_op jit(solution)/shard_map/pack/pallas_call | solution.py:102
  42.3 5.1 %all-to-all-start.1 = ((bf16[8,1040,128]{2,1,0:T(8,128)(2,1)}), bf16[8,1040,128]{2,1,0:T(8,128)(2,1)S(1)}, u32[]{:S(2)}, u32[]{:S(2)}) async-start(bf16[8,1040,128]{2,1,0:T(8,128)(2,1)} %pack.1), calls=%async_computation.1 | async-start | bytes 4259840 | tf_op jit(solution)/shard_map/all_to_all | solution.py:287
  47.4 2.5 %collective-permute-start.6 = (bf16[256,256]{1,0:T(8,128)(2,1)S(1)}, bf16[256,256]{1,0:T(8,128)(2,1)S(1)}, u32[]{:S(2)}, u32[]{:S(2)}) collective-permute-start(bf16[256,256]{1,0:T(8,128)(2,1)S(1)} %constant_dynamic-update-slice_fusion.refs_3_), channel_id=1, source_target_pairs={{0,4},{4,8},{8,12},{12,16},{16,20},{20,24},{24,28},{28,0},{1,5},{5... | collective-permute-start | bytes 393224 | tf_op jit(solution)/shard_map/ppermute | solution.py:260
  49.9 0.8 collective-permute-start.10
  50.8 3.3 %collective-permute-done.6.refs_1_ = bf16[256,256]{1,0:T(8,128)(2,1)S(1)} collective-permute-done((bf16[256,256]{1,0:T(8,128)(2,1)S(1)}, bf16[256,256]{1,0:T(8,128)(2,1)S(1)}, u32[]{:S(2)}, u32[]{:S(2)}) %collective-permute-start.6) | collective-permute-done | bytes 131104 | tf_op jit(solution)/shard_map/ppermute | solution.py:260
  54.1 0.8 collective-permute-start.7
  54.9 0.0 collective-permute-done.10.refs_2_
  54.9 2.4 %collective-permute-start.11 = (bf16[256,256]{1,0:T(8,128)(2,1)S(1)}, bf16[256,256]{1,0:T(8,128)(2,1)S(1)}, u32[]{:S(2)}, u32[]{:S(2)}) collective-permute-start(bf16[256,256]{1,0:T(8,128)(2,1)S(1)} %collective-permute-done.10.refs_2_), channel_id=1, source_target_pairs={{0,28},{4,0},{8,4},{12,8},{16,12},{20,16},{24,20},{28,24},{1,29},{... | collective-permute-start | bytes 393224 | tf_op jit(solution)/shard_map/ppermute | solution.py:260
  57.3 2.9 %collective-permute-done.7.refs_3_ = bf16[256,256]{1,0:T(8,128)(2,1)S(1)} collective-permute-done((bf16[256,256]{1,0:T(8,128)(2,1)S(1)}, bf16[256,256]{1,0:T(8,128)(2,1)S(1)}, u32[]{:S(2)}, u32[]{:S(2)}) %collective-permute-start.7) | collective-permute-done | bytes 131104 | tf_op jit(solution)/shard_map/ppermute | solution.py:260
  60.3 0.0 collective-permute-start.8
  60.3 0.0 collective-permute-done.11.refs_0_
  60.3 3.2 %collective-permute-start.12 = (bf16[256,256]{1,0:T(8,128)(2,1)S(1)}, bf16[256,256]{1,0:T(8,128)(2,1)S(1)}, u32[]{:S(2)}, u32[]{:S(2)}) collective-permute-start(bf16[256,256]{1,0:T(8,128)(2,1)S(1)} %collective-permute-done.11.refs_0_), channel_id=1, source_target_pairs={{0,28},{4,0},{8,4},{12,8},{16,12},{20,16},{24,20},{28,24},{1,29},{... | collective-permute-start | bytes 393224 | tf_op jit(solution)/shard_map/ppermute | solution.py:260
  63.5 2.9 %collective-permute-done.8.refs_1_ = bf16[256,256]{1,0:T(8,128)(2,1)S(1)} collective-permute-done((bf16[256,256]{1,0:T(8,128)(2,1)S(1)}, bf16[256,256]{1,0:T(8,128)(2,1)S(1)}, u32[]{:S(2)}, u32[]{:S(2)}) %collective-permute-start.8) | collective-permute-done | bytes 131104 | tf_op jit(solution)/shard_map/ppermute | solution.py:260
  66.5 0.0 collective-permute-start.9
  66.5 0.0 collective-permute-done.12.refs_2_
  66.5 6.2 %collective-permute-done.9.refs_0_ = bf16[256,256]{1,0:T(8,128)(2,1)S(1)} collective-permute-done((bf16[256,256]{1,0:T(8,128)(2,1)S(1)}, bf16[256,256]{1,0:T(8,128)(2,1)S(1)}, u32[]{:S(2)}, u32[]{:S(2)}) %collective-permute-start.9) | collective-permute-done | bytes 131104 | tf_op jit(solution)/shard_map/ppermute | solution.py:260
  72.6 4.2 %all-to-all-done.1.pay_ref = bf16[8,1040,128]{2,1,0:T(8,128)(2,1)S(1)} async-done(((bf16[8,1040,128]{2,1,0:T(8,128)(2,1)}), bf16[8,1040,128]{2,1,0:T(8,128)(2,1)S(1)}, u32[]{:S(2)}, u32[]{:S(2)}) %all-to-all-start.1) | async-done | bytes 2129952 | tf_op jit(solution)/shard_map/all_to_all | solution.py:287
  76.9 12.0 %far.1 = (bf16[8,256,128]{2,1,0:T(8,128)(2,1)S(1)}, f32[8,8,256]{2,1,0:T(8,128)S(1)}, f32[8,128,256]{2,1,0:T(8,128)S(1)}, bf16[2,256,128]{2,1,0:T(8,128)(2,1)S(1...) custom-call(bf16[8,1040,128]{2,1,0:T(8,128)(2,1)S(1)} %all-to-all-done.1.pay, ...), custom_call_target="tpu_custom_call" | custom-call | flops 15032385536 | bytes 4194304 | tf_op jit(solution)/shard_map/far/pallas_call | solution.py:215
  88.9 1.7 %collective-permute-start.13 = (bf16[2,256,128]{2,1,0:T(8,128)(2,1)S(1)}, bf16[2,256,128]{2,1,0:T(8,128)(2,1)S(1)}, u32[]{:S(2)}, u32[]{:S(2)}) collective-permute-start(bf16[2,256,128]{2,1,0:T(8,128)(2,1)S(1)} %get-tuple-element.36), channel_id=1, source_target_pairs={{0,16},{4,20},{8,24},{12,28},{16,0},{20,4},{24,8},{28,12},{1,17},{... | collective-permute-start | bytes 393224 | tf_op jit(solution)/shard_map/ppermute | solution.py:260
  90.6 3.4 %collective-permute-start.14 = (bf16[2,256,128]{2,1,0:T(8,128)(2,1)S(1)}, bf16[2,256,128]{2,1,0:T(8,128)(2,1)S(1)}, u32[]{:S(2)}, u32[]{:S(2)}) collective-permute-start(bf16[2,256,128]{2,1,0:T(8,128)(2,1)S(1)} %get-tuple-element.37), channel_id=1, source_target_pairs={{0,20},{4,24},{8,28},{12,0},{16,4},{20,8},{24,12},{28,16},{1,21},{... | collective-permute-start | bytes 393224 | tf_op jit(solution)/shard_map/ppermute | solution.py:260
  94.0 0.4 collective-permute-start.15
  94.4 4.0 %collective-permute-start.16 = (bf16[2,256,128]{2,1,0:T(8,128)(2,1)S(1)}, bf16[2,256,128]{2,1,0:T(8,128)(2,1)S(1)}, u32[]{:S(2)}, u32[]{:S(2)}) collective-permute-start(bf16[2,256,128]{2,1,0:T(8,128)(2,1)S(1)} %get-tuple-element.39), channel_id=1, source_target_pairs={{0,24},{4,28},{8,0},{12,4},{16,8},{20,12},{24,16},{28,20},{1,25},{... | collective-permute-start | bytes 393224 | tf_op jit(solution)/shard_map/ppermute | solution.py:260
  98.5 11.4 %near.1 = (bf16[8,128,256]{2,1,0:T(8,128)(2,1)}, bf16[2,256,128]{2,1,0:T(8,128)(2,1)S(1)}, bf16[2,256,128]{2,1,0:T(8,128)(2,1)S(1)}, bf16[2,256,128]{2,1,0:T(8,128)(2,1)S(1)}, bf16[2,256,128]{2,1,0:T(8,128)(2,1)S(1)}) custom-call(bf16[8,1040,128]{2,1,0:T(8,128)(2,1)S(1)} %all-to-all-done.1.pay_ref, bf16[256,256]{1,0:T(8,128)(2,1)S(1)} %collective-permute-done.11.refs_0_, ...), custom_call_target="tpu_custom_call" | custom-call | flops 15032385536 | bytes 4194304 | tf_op jit(solution)/shard_map/near/pallas_call | solution.py:215
  109.9 0.7 copy-done.3
  110.5 0.6 copy-done.4
  111.2 0.0 collective-permute-done.13.refs_0_
  111.2 0.0 collective-permute-done.14.refs_1_
  111.2 0.0 collective-permute-done.15.refs_2_
  111.2 0.0 collective-permute-done.16.refs_3_
  111.2 7.3 %all-to-all-start.2 = ((bf16[8,128,256]{2,1,0:T(8,128)(2,1)}), bf16[8,128,256]{2,1,0:T(8,128)(2,1)S(1)}, u32[]{:S(2)}, u32[]{:S(2)}) async-start(bf16[8,128,256]{2,1,0:T(8,128)(2,1)} %get-tuple-element.52), calls=%async_computation.2 | async-start | bytes 1048576 | tf_op jit(solution)/shard_map/all_to_all | solution.py:293
  118.5 3.4 %collective-permute-start.17 = (bf16[2,256,128]{2,1,0:T(8,128)(2,1)}, bf16[2,256,128]{2,1,0:T(8,128)(2,1)S(1)}, u32[]{:S(2)}, u32[]{:S(2)}) collective-permute-start(bf16[2,256,128]{2,1,0:T(8,128)(2,1)} %copy-done.4), channel_id=1, source_target_pairs={{0,8},{4,12},{8,16},{12,20},{16,24},{20,28},{24,0},{28,4},{1,9},{5... | collective-permute-start | bytes 393224 | tf_op jit(solution)/shard_map/ppermute | solution.py:260
  121.9 0.0 collective-permute-start.18
  121.9 2.0 %collective-permute-start.19 = (bf16[2,256,128]{2,1,0:T(8,128)(2,1)S(1)}, bf16[2,256,128]{2,1,0:T(8,128)(2,1)S(1)}, u32[]{:S(2)}, u32[]{:S(2)}) collective-permute-start(bf16[2,256,128]{2,1,0:T(8,128)(2,1)S(1)} %get-tuple-element.50), channel_id=1, source_target_pairs={{0,4},{4,8},{8,12},{12,16},{16,20},{20,24},{24,28},{28,0},{1,5},{5... | collective-permute-start | bytes 393224 | tf_op jit(solution)/shard_map/ppermute | solution.py:260
  123.9 4.3 %collective-permute-done.17.refs_4_ = bf16[2,256,128]{2,1,0:T(8,128)(2,1)S(1)} collective-permute-done((bf16[2,256,128]{2,1,0:T(8,128)(2,1)}, bf16[2,256,128]{2,1,0:T(8,128)(2,1)S(1)}, u32[]{:S(2)}, u32[]{:S(2)}) %collective-permute-start.17) | collective-permute-done | bytes 131104 | tf_op jit(solution)/shard_map/ppermute | solution.py:260
  128.3 0.0 collective-permute-done.18.refs_5_
  128.3 1.5 %collective-permute-done.19.refs_6_ = bf16[2,256,128]{2,1,0:T(8,128)(2,1)S(1)} collective-permute-done((bf16[2,256,128]{2,1,0:T(8,128)(2,1)S(1)}, bf16[2,256,128]{2,1,0:T(8,128)(2,1)S(1)}, u32[]{:S(2)}, u32[]{:S(2)}) %collective-permute-start.19) | collective-permute-done | bytes 131104 | tf_op jit(solution)/shard_map/ppermute | solution.py:260
  129.8 0.0 all-to-all-done.2.refs_8_
  129.8 0.9 finish.1
  (26 shorter events, 0.2 us)
Async XLA Ops:
  0.6 26.7 %copy-start.11 = (s32[1,64]{1,0:T(1,128)S(1)}, s32[1,64]{1,0:T(1,128)}, u32[]{:S(2)}) copy-start(s32[1,64]{1,0:T(1,128)} %param.19) | copy-start | bytes 772
  0.6 27.1 %copy-start.10 = (f32[2,256]{1,0:T(2,128)S(1)}, f32[2,256]{1,0:T(2,128)}, u32[]{:S(2)}) copy-start(f32[2,256]{1,0:T(2,128)} %param.14) | copy-start | bytes 6148
  0.7 39.1 %copy-start = (bf16[256,128]{1,0:T(8,128)(2,1)S(1)}, bf16[256,128]{1,0:T(8,128)(2,1)}, u32[]{:S(2)}) copy-start(bf16[256,128]{1,0:T(8,128)(2,1)} %q_ref.1) | copy-start | bytes 196612
  0.7 39.1 %copy-start.1 = (bf16[256,128]{1,0:T(8,128)(2,1)S(1)}, bf16[256,128]{1,0:T(8,128)(2,1)}, u32[]{:S(2)}) copy-start(bf16[256,128]{1,0:T(8,128)(2,1)} %out_ref.1) | copy-start | bytes 196612
  0.7 9.8 %collective-permute-start.1 = (bf16[128,1024]{1,0:T(8,128)(2,1)}, bf16[128,1024]{1,0:T(8,128)(2,1)S(1)}, u32[]{:S(2)}, u32[]{:S(2)}) collective-permute-start(bf16[128,1024]{1,0:T(8,128)(2,1)} %refs_3_.1), channel_id=1, source_target_pairs={{0,2},{2,0},{1,3},{3,1},{4,6},{6,4},{5,7},{7,5},{8,10},{10,8},{9,1... | collective-permute-start | bytes 786440 | tf_op jit(solution)/shard_map/ppermute | solution.py:256
  4.0 6.6 %collective-permute-start = (bf16[128,1024]{1,0:T(8,128)(2,1)}, bf16[128,1024]{1,0:T(8,128)(2,1)S(1)}, u32[]{:S(2)}, u32[]{:S(2)}) collective-permute-start(bf16[128,1024]{1,0:T(8,128)(2,1)} %refs_3_.1), channel_id=1, source_target_pairs={{0,1},{1,0},{2,3},{3,2},{4,5},{5,4},{6,7},{7,6},{8,9},{9,8},{10,11... | collective-permute-start | bytes 786440 | tf_op jit(solution)/shard_map/ppermute | solution.py:256
  10.5 1.5 %copy-start.5 = (bf16[128,1024]{1,0:T(8,128)(2,1)}, bf16[128,1024]{1,0:T(8,128)(2,1)S(1)}, u32[]{:S(2)}) copy-start(bf16[128,1024]{1,0:T(8,128)(2,1)S(1)} %collective-permute-done.1.refs_5_) | copy-start | bytes 786436
  10.5 1.5 %collective-permute-start.2 = (bf16[128,1024]{1,0:T(8,128)(2,1)S(1)}, bf16[128,1024]{1,0:T(8,128)(2,1)S(1)}, u32[]{:S(2)}, u32[]{:S(2)}) collective-permute-start(bf16[128,1024]{1,0:T(8,128)(2,1)S(1)} %collective-permute-done.1.refs_5_), channel_id=1, source_target_pairs={{0,1},{1,0},{2,3},{3,2},{4,5},{5,4},{6,7},{7,6},{8,9},{9,8},{10,11... | collective-permute-start | bytes 786440 | tf_op jit(solution)/shard_map/ppermute | solution.py:256
  10.5 1.5 %copy-start.6 = (bf16[128,1024]{1,0:T(8,128)(2,1)}, bf16[128,1024]{1,0:T(8,128)(2,1)S(1)}, u32[]{:S(2)}) copy-start(bf16[128,1024]{1,0:T(8,128)(2,1)S(1)} %collective-permute-done.refs_4_) | copy-start | bytes 786436
  12.1 0.7 copy-start.7
  15.9 23.9 %all-to-all-start = ((bf16[32,32,128]{2,1,0:T(8,128)(2,1)}), bf16[32,32,128]{2,1,0:T(8,128)(2,1)S(1)}, u32[]{:S(2)}, u32[]{:S(2)}) async-start(bf16[32,32,128]{2,1,0:T(8,128)(2,1)} %bitcast.4), calls=%async_computation | async-start | bytes 524288 | tf_op jit(solution)/shard_map/all_to_all | solution.py:272
  27.8 3.7 %collective-permute-start.3 = (bf16[256,128]{1,0:T(8,128)(2,1)}, bf16[256,128]{1,0:T(8,128)(2,1)S(1)}, u32[]{:S(2)}, u32[]{:S(2)}) collective-permute-start(bf16[256,128]{1,0:T(8,128)(2,1)} %get-tuple-element.30), channel_id=1, source_target_pairs={{0,1},{1,0},{2,3},{3,2},{4,5},{5,4},{6,7},{7,6},{8,9},{9,8},{10,11... | collective-permute-start | bytes 196616 | tf_op jit(solution)/shard_map/ppermute | solution.py:270
  28.2 7.1 %collective-permute-start.4 = (bf16[256,128]{1,0:T(8,128)(2,1)}, bf16[256,128]{1,0:T(8,128)(2,1)S(1)}, u32[]{:S(2)}, u32[]{:S(2)}) collective-permute-start(bf16[256,128]{1,0:T(8,128)(2,1)} %get-tuple-element.31), channel_id=1, source_target_pairs={{0,2},{1,3},{2,0},{3,1},{4,6},{5,7},{6,4},{7,5},{8,10},{9,11},{10,... | collective-permute-start | bytes 196616 | tf_op jit(solution)/shard_map/ppermute | solution.py:270
  31.4 7.3 %collective-permute-start.5 = (bf16[256,128]{1,0:T(8,128)(2,1)}, bf16[256,128]{1,0:T(8,128)(2,1)S(1)}, u32[]{:S(2)}, u32[]{:S(2)}) collective-permute-start(bf16[256,128]{1,0:T(8,128)(2,1)} %get-tuple-element.32), channel_id=1, source_target_pairs={{0,3},{1,2},{2,1},{3,0},{4,7},{5,6},{6,5},{7,4},{8,11},{9,10},{10,... | collective-permute-start | bytes 196616 | tf_op jit(solution)/shard_map/ppermute | solution.py:270
  39.8 0.8 copy-start.2
  42.3 5.1 %copy-start.8 = (bf16[256,128]{1,0:T(8,128)(2,1)S(1)}, bf16[256,128]{1,0:T(8,128)(2,1)}, u32[]{:S(2)}) copy-start(bf16[256,128]{1,0:T(8,128)(2,1)} %param.11) | copy-start | bytes 196612
  42.3 5.1 %copy-start.9 = (bf16[256,128]{1,0:T(8,128)(2,1)S(1)}, bf16[256,128]{1,0:T(8,128)(2,1)}, u32[]{:S(2)}) copy-start(bf16[256,128]{1,0:T(8,128)(2,1)} %param.12) | copy-start | bytes 196612
  42.3 34.6 %all-to-all-start.1 = ((bf16[8,1040,128]{2,1,0:T(8,128)(2,1)}), bf16[8,1040,128]{2,1,0:T(8,128)(2,1)S(1)}, u32[]{:S(2)}, u32[]{:S(2)}) async-start(bf16[8,1040,128]{2,1,0:T(8,128)(2,1)} %pack.1), calls=%async_computation.1 | async-start | bytes 4259840 | tf_op jit(solution)/shard_map/all_to_all | solution.py:287
  47.4 6.7 %collective-permute-start.6 = (bf16[256,256]{1,0:T(8,128)(2,1)S(1)}, bf16[256,256]{1,0:T(8,128)(2,1)S(1)}, u32[]{:S(2)}, u32[]{:S(2)}) collective-permute-start(bf16[256,256]{1,0:T(8,128)(2,1)S(1)} %constant_dynamic-update-slice_fusion.refs_3_), channel_id=1, source_target_pairs={{0,4},{4,8},{8,12},{12,16},{16,20},{20,24},{24,28},{28,0},{1,5},{5... | collective-permute-start | bytes 393224 | tf_op jit(solution)/shard_map/ppermute | solution.py:260
  49.9 5.0 %collective-permute-start.10 = (bf16[256,256]{1,0:T(8,128)(2,1)S(1)}, bf16[256,256]{1,0:T(8,128)(2,1)S(1)}, u32[]{:S(2)}, u32[]{:S(2)}) collective-permute-start(bf16[256,256]{1,0:T(8,128)(2,1)S(1)} %constant_dynamic-update-slice_fusion.refs_3_), channel_id=1, source_target_pairs={{0,28},{4,0},{8,4},{12,8},{16,12},{20,16},{24,20},{28,24},{1,29},{... | collective-permute-start | bytes 393224 | tf_op jit(solution)/shard_map/ppermute | solution.py:260
  54.1 6.2 %collective-permute-start.7 = (bf16[256,256]{1,0:T(8,128)(2,1)S(1)}, bf16[256,256]{1,0:T(8,128)(2,1)S(1)}, u32[]{:S(2)}, u32[]{:S(2)}) collective-permute-start(bf16[256,256]{1,0:T(8,128)(2,1)S(1)} %collective-permute-done.6.refs_1_), channel_id=1, source_target_pairs={{0,4},{4,8},{8,12},{12,16},{16,20},{20,24},{24,28},{28,0},{1,5},{5... | collective-permute-start | bytes 393224 | tf_op jit(solution)/shard_map/ppermute | solution.py:260
  54.9 5.4 %collective-permute-start.11 = (bf16[256,256]{1,0:T(8,128)(2,1)S(1)}, bf16[256,256]{1,0:T(8,128)(2,1)S(1)}, u32[]{:S(2)}, u32[]{:S(2)}) collective-permute-start(bf16[256,256]{1,0:T(8,128)(2,1)S(1)} %collective-permute-done.10.refs_2_), channel_id=1, source_target_pairs={{0,28},{4,0},{8,4},{12,8},{16,12},{20,16},{24,20},{28,24},{1,29},{... | collective-permute-start | bytes 393224 | tf_op jit(solution)/shard_map/ppermute | solution.py:260
  60.3 6.2 %collective-permute-start.8 = (bf16[256,256]{1,0:T(8,128)(2,1)S(1)}, bf16[256,256]{1,0:T(8,128)(2,1)S(1)}, u32[]{:S(2)}, u32[]{:S(2)}) collective-permute-start(bf16[256,256]{1,0:T(8,128)(2,1)S(1)} %collective-permute-done.7.refs_3_), channel_id=1, source_target_pairs={{0,4},{4,8},{8,12},{12,16},{16,20},{20,24},{24,28},{28,0},{1,5},{5... | collective-permute-start | bytes 393224 | tf_op jit(solution)/shard_map/ppermute | solution.py:260
  60.3 6.2 %collective-permute-start.12 = (bf16[256,256]{1,0:T(8,128)(2,1)S(1)}, bf16[256,256]{1,0:T(8,128)(2,1)S(1)}, u32[]{:S(2)}, u32[]{:S(2)}) collective-permute-start(bf16[256,256]{1,0:T(8,128)(2,1)S(1)} %collective-permute-done.11.refs_0_), channel_id=1, source_target_pairs={{0,28},{4,0},{8,4},{12,8},{16,12},{20,16},{24,20},{28,24},{1,29},{... | collective-permute-start | bytes 393224 | tf_op jit(solution)/shard_map/ppermute | solution.py:260
  66.5 6.2 %collective-permute-start.9 = (bf16[256,256]{1,0:T(8,128)(2,1)S(1)}, bf16[256,256]{1,0:T(8,128)(2,1)S(1)}, u32[]{:S(2)}, u32[]{:S(2)}) collective-permute-start(bf16[256,256]{1,0:T(8,128)(2,1)S(1)} %collective-permute-done.8.refs_1_), channel_id=1, source_target_pairs={{0,4},{4,8},{8,12},{12,16},{16,20},{20,24},{24,28},{28,0},{1,5},{5... | collective-permute-start | bytes 393224 | tf_op jit(solution)/shard_map/ppermute | solution.py:260
  88.9 22.3 %collective-permute-start.13 = (bf16[2,256,128]{2,1,0:T(8,128)(2,1)S(1)}, bf16[2,256,128]{2,1,0:T(8,128)(2,1)S(1)}, u32[]{:S(2)}, u32[]{:S(2)}) collective-permute-start(bf16[2,256,128]{2,1,0:T(8,128)(2,1)S(1)} %get-tuple-element.36), channel_id=1, source_target_pairs={{0,16},{4,20},{8,24},{12,28},{16,0},{20,4},{24,8},{28,12},{1,17},{... | collective-permute-start | bytes 393224 | tf_op jit(solution)/shard_map/ppermute | solution.py:260
  90.6 20.6 %collective-permute-start.14 = (bf16[2,256,128]{2,1,0:T(8,128)(2,1)S(1)}, bf16[2,256,128]{2,1,0:T(8,128)(2,1)S(1)}, u32[]{:S(2)}, u32[]{:S(2)}) collective-permute-start(bf16[2,256,128]{2,1,0:T(8,128)(2,1)S(1)} %get-tuple-element.37), channel_id=1, source_target_pairs={{0,20},{4,24},{8,28},{12,0},{16,4},{20,8},{24,12},{28,16},{1,21},{... | collective-permute-start | bytes 393224 | tf_op jit(solution)/shard_map/ppermute | solution.py:260
  94.0 17.2 %collective-permute-start.15 = (bf16[2,256,128]{2,1,0:T(8,128)(2,1)S(1)}, bf16[2,256,128]{2,1,0:T(8,128)(2,1)S(1)}, u32[]{:S(2)}, u32[]{:S(2)}) collective-permute-start(bf16[2,256,128]{2,1,0:T(8,128)(2,1)S(1)} %get-tuple-element.38), channel_id=1, source_target_pairs={{0,12},{4,16},{8,20},{12,24},{16,28},{20,0},{24,4},{28,8},{1,13},{... | collective-permute-start | bytes 393224 | tf_op jit(solution)/shard_map/ppermute | solution.py:260
  94.4 16.8 %collective-permute-start.16 = (bf16[2,256,128]{2,1,0:T(8,128)(2,1)S(1)}, bf16[2,256,128]{2,1,0:T(8,128)(2,1)S(1)}, u32[]{:S(2)}, u32[]{:S(2)}) collective-permute-start(bf16[2,256,128]{2,1,0:T(8,128)(2,1)S(1)} %get-tuple-element.39), channel_id=1, source_target_pairs={{0,24},{4,28},{8,0},{12,4},{16,8},{20,12},{24,16},{28,20},{1,25},{... | collective-permute-start | bytes 393224 | tf_op jit(solution)/shard_map/ppermute | solution.py:260
  109.9 0.7 copy-start.3
  110.5 0.6 copy-start.4
  111.2 18.6 %all-to-all-start.2 = ((bf16[8,128,256]{2,1,0:T(8,128)(2,1)}), bf16[8,128,256]{2,1,0:T(8,128)(2,1)S(1)}, u32[]{:S(2)}, u32[]{:S(2)}) async-start(bf16[8,128,256]{2,1,0:T(8,128)(2,1)} %get-tuple-element.52), calls=%async_computation.2 | async-start | bytes 1048576 | tf_op jit(solution)/shard_map/all_to_all | solution.py:293
  118.5 9.8 %collective-permute-start.17 = (bf16[2,256,128]{2,1,0:T(8,128)(2,1)}, bf16[2,256,128]{2,1,0:T(8,128)(2,1)S(1)}, u32[]{:S(2)}, u32[]{:S(2)}) collective-permute-start(bf16[2,256,128]{2,1,0:T(8,128)(2,1)} %copy-done.4), channel_id=1, source_target_pairs={{0,8},{4,12},{8,16},{12,20},{16,24},{20,28},{24,0},{28,4},{1,9},{5... | collective-permute-start | bytes 393224 | tf_op jit(solution)/shard_map/ppermute | solution.py:260
  121.9 6.4 %collective-permute-start.18 = (bf16[2,256,128]{2,1,0:T(8,128)(2,1)}, bf16[2,256,128]{2,1,0:T(8,128)(2,1)S(1)}, u32[]{:S(2)}, u32[]{:S(2)}) collective-permute-start(bf16[2,256,128]{2,1,0:T(8,128)(2,1)} %copy-done.3), channel_id=1, source_target_pairs={{0,28},{4,0},{8,4},{12,8},{16,12},{20,16},{24,20},{28,24},{1,29},{... | collective-permute-start | bytes 393224 | tf_op jit(solution)/shard_map/ppermute | solution.py:260
  121.9 7.9 %collective-permute-start.19 = (bf16[2,256,128]{2,1,0:T(8,128)(2,1)S(1)}, bf16[2,256,128]{2,1,0:T(8,128)(2,1)S(1)}, u32[]{:S(2)}, u32[]{:S(2)}) collective-permute-start(bf16[2,256,128]{2,1,0:T(8,128)(2,1)S(1)} %get-tuple-element.50), channel_id=1, source_target_pairs={{0,4},{4,8},{8,12},{12,16},{16,20},{20,24},{24,28},{28,0},{1,5},{5... | collective-permute-start | bytes 393224 | tf_op jit(solution)/shard_map/ppermute | solution.py:260

commit v3 on v2

--- a/solution.py
+++ b/solution.py
@@ -11,10 +11,9 @@
 HD = 64
 BLK = 4
 SIDE = 8
-PAIR = 2
-HALF = 4
-FAR = (4, 3, -3, 2)
-NEAR = (-2, 1, -1, 0)
+PAIR = 4
+FAR = (4, 3, -3)
+NEAR = (2, -2, 1, -1, 0)
 VMEM = 24 << 20
 LARGE = 60 << 20
 R = ("yl", "x")
@@ -132,16 +131,17 @@
 
 
 def attention_kernel(far, pay_ref, *refs):
-    kv_refs, refs = refs[:HALF], refs[HALF:]
+    count = len(FAR if far else NEAR)
+    kv_refs, refs = refs[:count], refs[count:]
     if far:
-        shared, vk_refs, (kt_ref, dv_acc, dk_acc) = refs[:3], refs[3 : 3 + HALF], refs[3 + HALF :]
+        shared, vk_refs, (kt_ref, dv_acc, dk_acc) = refs[:3], refs[3 : 3 + count], refs[3 + count :]
         dq_out = None
     else:
         shared, dq_out, refs = refs[:3], refs[3], refs[4:]
-        vk_refs, (kt_ref, dv_acc, dk_acc) = refs[:HALF], refs[HALF:]
+        vk_refs, (kt_ref, dv_acc, dk_acc) = refs[:count], refs[count:]
     dv_acc[...] = jnp.zeros_like(dv_acc)
     dk_acc[...] = jnp.zeros_like(dk_acc)
-    for t in range(HALF):
+    for t in range(count):
         kt_ref[:, t * 256 : (t + 1) * 256] = kv_refs[t][:, 0:128].astype(f32).T.astype(bf16)
 
     def step_of(step, carry):
@@ -149,7 +149,7 @@
         return carry
 
     lax.fori_loop(0, SIDE // PAIR, step_of, 0)
-    for t in range(HALF):
+    for t in range(count):
         vk_refs[t][0] = dv_acc[t * 256 : (t + 1) * 256, :].astype(bf16)
         vk_refs[t][1] = dk_acc[t * 256 : (t + 1) * 256, :].astype(bf16)
 
@@ -178,9 +178,9 @@
 
     dq = [jnp.zeros((HD, 256), f32) for _ in chains]
     later = scores_of(0)
-    for t in range(HALF):
+    for t in range(len(kv_refs)):
         now = later
-        if t + 1 < HALF:
+        if t + 1 < len(kv_refs):
             later = scores_of(t + 1)
         keys = slice(t * 256, (t + 1) * 256)
         probs, d_scores = [], []
@@ -214,11 +214,11 @@
     ins = [pay, *kv] + ([] if far else list(shared))
     out = pl.pallas_call(
         functools.partial(attention_kernel, far),
-        out_shape=outs + [jax.ShapeDtypeStruct((2, 256, 128), bf16)] * HALF,
+        out_shape=outs + [jax.ShapeDtypeStruct((2, 256, 128), bf16)] * len(kv),
         scratch_shapes=[
-            pltpu.VMEM((128, HALF * 256), bf16),
-            pltpu.VMEM((HALF * 256, 128), f32),
-            pltpu.VMEM((HALF * 256, 128), f32),
+            pltpu.VMEM((128, len(kv) * 256), bf16),
+            pltpu.VMEM((len(kv) * 256, 128), f32),
+            pltpu.VMEM((len(kv) * 256, 128), f32),
         ],
         compiler_params=pltpu.CompilerParams(vmem_limit_bytes=VMEM),
         cost_estimate=pl.CostEstimate(flops=14 << 30, bytes_accessed=1 << 22, transcendentals=1 << 22),

time: 131 us -> 130 us (level)
  starting transfers between devices: 55.5 us -> 53.4 us
    ppermute x14, starting transfers between devices: 24.8 us -> 22.7 us  [shift(): return lax.ppermute(x, axis, [(i, (i + by) % size) for i in range(size)])]
    unnamed x25 -> x27, local copies, waits for them, and re-layouts: 2.87 us -> 3.57 us
  transfers between devices with their start and end apart: 23 -> 23, of which waited for: 12 -> 13; matrix products, arithmetic and copies ran while one was open for 0% -> 0% of each run, Pallas kernels for 9% -> 10%
where the time goes in v3:
time: 130 us; the launch traced here: 129 us
  starting transfers between devices  53.4 us (41%)
  waiting for transfers between devices  42.9 us (33%)
  Pallas kernels  28.3 us (22%)
  local copies, waits for them, and re-layouts  4.07 us (3%)
    ppermute x14, starting transfers between devices, shift(): return lax.ppermute(x, axis, [(i, (i + by) % size) for i in range(size)])  22.7 us
    pallas_call x2, Pallas kernels, attention(): pl.pallas_call(functools.partial(attention_kernel, far), out_shape=outs +...  22.6 us
    ppermute x14, waiting for transfers between devices, shift(): return lax.ppermute(x, axis, [(i, (i + by) % size) for i in range(size)])  22.3 us
    all_to_all x1, starting transfers between devices, body(): lax.all_to_all(part.reshape(4 * SIDE, 32, width), T + (C,), 0, 0, tiled=T...  11.5 us
    ppermute x3, waiting for transfers between devices, flip(): return lax.ppermute(x, axis, [(0, 1), (1, 0)])  8.08 us
    all_to_all x1, starting transfers between devices, body(): dq = lax.all_to_all(dq, R, 0, 0, tiled=True)  7.28 us
    ppermute x3, waiting for transfers between devices, body(): lax.ppermute(us[i], T, [(t, t ^ i) for t in range(4)])  7.14 us
    all_to_all x1, starting transfers between devices, body(): pay = lax.all_to_all(pay, R, 0, 0, tiled=True)  5.07 us
  transfers between devices with their start and end apart: 23, of which 13 were waited for; matrix products, arithmetic and copies ran while one was open for 0% of the time, Pallas kernels for 10%

profile of v3, /device:TPU:2, one launch (start us, length us, event | category | flops | bytes accessed | tf_op | source)
XLA Modules:
  0.0 129.5 jit_solution(3446549821978485642)
XLA Ops:
  0.6 0.0 copy-start.12
  0.6 0.0 copy-start.11
  0.7 0.0 copy-start
  0.7 3.3 %collective-permute-start.1 = (bf16[128,1024]{1,0:T(8,128)(2,1)}, bf16[128,1024]{1,0:T(8,128)(2,1)S(1)}, u32[]{:S(2)}, u32[]{:S(2)}) collective-permute-start(bf16[128,1024]{1,0:T(8,128)(2,1)} %refs_3_.1), channel_id=1, source_target_pairs={{0,2},{2,0},{1,3},{3,1},{4,6},{6,4},{5,7},{7,5},{8,10},{10,8},{9,1... | collective-permute-start | bytes 786440 | tf_op jit(solution)/shard_map/ppermute | solution.py:256
  4.0 0.0 collective-permute-start
  4.0 6.6 %collective-permute-done.1.refs_5_ = bf16[128,1024]{1,0:T(8,128)(2,1)S(1)} collective-permute-done((bf16[128,1024]{1,0:T(8,128)(2,1)}, bf16[128,1024]{1,0:T(8,128)(2,1)S(1)}, u32[]{:S(2)}, u32[]{:S(2)}) %collective-permute-start.1) | collective-permute-done | bytes 262176 | tf_op jit(solution)/shard_map/ppermute | solution.py:256
  10.5 0.0 collective-permute-start.2
  10.5 0.0 collective-permute-done.refs_4_
  10.5 1.5 %collective-permute-done.2.refs_6_ = bf16[128,1024]{1,0:T(8,128)(2,1)S(1)} collective-permute-done((bf16[128,1024]{1,0:T(8,128)(2,1)S(1)}, bf16[128,1024]{1,0:T(8,128)(2,1)S(1)}, u32[]{:S(2)}, u32[]{:S(2)}) %collective-permute-start.2) | collective-permute-done | bytes 262176 | tf_op jit(solution)/shard_map/ppermute | solution.py:256
  12.1 0.7 copy-done.8
  12.8 3.1 %project.1 = (bf16[4,256,128]{2,1,0:T(8,128)(2,1)}, bf16[256,128]{1,0:T(8,128)(2,1)}, bf16[256,128]{1,0:T(8,128)(2,1)}, bf16[256,128]{1,0:T(8,128)(2,1)}, bf16[256,128]{1,0:T(8,128)(2,1)}) custom-call(s32[1]{0:T(128)} %bitcast.tile_ref, bf16[256,256]{1,0:T(8,128)(2,1)} %refs_0_.1, bf16[256,256]{1,0:T(8,128)(2,1)} %refs_1_.1, bf16[1024,256]{1,0:T(8,128)(2,1)} %refs_2_.1, ...), custom_call_target="tpu_custom_call" | custom-call | tf_op jit(solution)/shard_map/project/pallas_call | solution.py:65
  15.9 11.5 %all-to-all-start = ((bf16[32,32,128]{2,1,0:T(8,128)(2,1)}), bf16[32,32,128]{2,1,0:T(8,128)(2,1)S(1)}, u32[]{:S(2)}, u32[]{:S(2)}) async-start(bf16[32,32,128]{2,1,0:T(8,128)(2,1)} %bitcast.4), calls=%async_computation | async-start | bytes 524288 | tf_op jit(solution)/shard_map/all_to_all | solution.py:272
  27.4 0.1 mul.20
  27.5 0.1 add.24
  27.6 0.1 add.25
  27.7 0.1 add.27
  27.8 0.4 collective-permute-start.3
  28.2 3.2 %collective-permute-start.4 = (bf16[256,128]{1,0:T(8,128)(2,1)}, bf16[256,128]{1,0:T(8,128)(2,1)S(1)}, u32[]{:S(2)}, u32[]{:S(2)}) collective-permute-start(bf16[256,128]{1,0:T(8,128)(2,1)} %get-tuple-element.30), channel_id=1, source_target_pairs={{0,2},{1,3},{2,0},{3,1},{4,6},{5,7},{6,4},{7,5},{8,10},{9,11},{10,... | collective-permute-start | bytes 196616 | tf_op jit(solution)/shard_map/ppermute | solution.py:270
  31.4 0.0 collective-permute-start.5
  31.5 0.1 concatenate.6.misc_ref
  31.5 0.0 collective-permute-done.3.u1_ref
  31.5 3.7 %collective-permute-done.4.u2_ref = bf16[256,128]{1,0:T(8,128)(2,1)S(1)} collective-permute-done((bf16[256,128]{1,0:T(8,128)(2,1)}, bf16[256,128]{1,0:T(8,128)(2,1)S(1)}, u32[]{:S(2)}, u32[]{:S(2)}) %collective-permute-start.4) | collective-permute-done | bytes 65568 | tf_op jit(solution)/shard_map/ppermute | solution.py:270
  35.2 3.4 %collective-permute-done.5.u3_ref = bf16[256,128]{1,0:T(8,128)(2,1)S(1)} collective-permute-done((bf16[256,128]{1,0:T(8,128)(2,1)}, bf16[256,128]{1,0:T(8,128)(2,1)S(1)}, u32[]{:S(2)}, u32[]{:S(2)}) %collective-permute-start.5) | collective-permute-done | bytes 65568 | tf_op jit(solution)/shard_map/ppermute | solution.py:270
  38.7 1.1 all-to-all-done
  39.8 0.8 copy-done.2
  40.7 1.7 %pack.1 = bf16[8,1040,128]{2,1,0:T(8,128)(2,1)} custom-call(bf16[4,256,128]{2,1,0:T(8,128)(2,1)S(1)} %bitcast.3, bf16[256,128]{1,0:T(8,128)(2,1)S(1)} %copy-done, bf16[256,128]{1,0:T(8,128)(2,1)S(1)} %copy-done.1, bf16[16,128]{1,0:T(8,128)(2,1)S(1)} %concatenate.6.misc_ref, bf16[256,128]{1,0:T(8,128)(2,1)S(1)} %copy-done.2, ...), custom_call_target="tpu_custom_call" | custom-call | tf_op jit(solution)/shard_map/pack/pallas_call | solution.py:101
  42.3 5.1 %all-to-all-start.1 = ((bf16[8,1040,128]{2,1,0:T(8,128)(2,1)}), bf16[8,1040,128]{2,1,0:T(8,128)(2,1)S(1)}, u32[]{:S(2)}, u32[]{:S(2)}) async-start(bf16[8,1040,128]{2,1,0:T(8,128)(2,1)} %pack.1), calls=%async_computation.1 | async-start | bytes 4259840 | tf_op jit(solution)/shard_map/all_to_all | solution.py:287
  47.5 2.5 %collective-permute-start.6 = (bf16[256,256]{1,0:T(8,128)(2,1)S(1)}, bf16[256,256]{1,0:T(8,128)(2,1)S(1)}, u32[]{:S(2)}, u32[]{:S(2)}) collective-permute-start(bf16[256,256]{1,0:T(8,128)(2,1)S(1)} %constant_dynamic-update-slice_fusion.refs_4_), channel_id=1, source_target_pairs={{0,4},{4,8},{8,12},{12,16},{16,20},{20,24},{24,28},{28,0},{1,5},{5... | collective-permute-start | bytes 393224 | tf_op jit(solution)/shard_map/ppermute | solution.py:260
  50.0 0.8 collective-permute-start.10
  50.8 3.3 %collective-permute-done.6.refs_2_ = bf16[256,256]{1,0:T(8,128)(2,1)S(1)} collective-permute-done((bf16[256,256]{1,0:T(8,128)(2,1)S(1)}, bf16[256,256]{1,0:T(8,128)(2,1)S(1)}, u32[]{:S(2)}, u32[]{:S(2)}) %collective-permute-start.6) | collective-permute-done | bytes 131104 | tf_op jit(solution)/shard_map/ppermute | solution.py:260
  54.1 0.8 collective-permute-start.7
  55.0 0.0 collective-permute-done.10.refs_3_
  55.0 2.4 %collective-permute-start.11 = (bf16[256,256]{1,0:T(8,128)(2,1)S(1)}, bf16[256,256]{1,0:T(8,128)(2,1)S(1)}, u32[]{:S(2)}, u32[]{:S(2)}) collective-permute-start(bf16[256,256]{1,0:T(8,128)(2,1)S(1)} %collective-permute-done.10.refs_3_), channel_id=1, source_target_pairs={{0,28},{4,0},{8,4},{12,8},{16,12},{20,16},{24,20},{28,24},{1,29},{... | collective-permute-start | bytes 393224 | tf_op jit(solution)/shard_map/ppermute | solution.py:260
  57.4 2.9 %collective-permute-done.7.refs_0_ = bf16[256,256]{1,0:T(8,128)(2,1)S(1)} collective-permute-done((bf16[256,256]{1,0:T(8,128)(2,1)S(1)}, bf16[256,256]{1,0:T(8,128)(2,1)S(1)}, u32[]{:S(2)}, u32[]{:S(2)}) %collective-permute-start.7) | collective-permute-done | bytes 131104 | tf_op jit(solution)/shard_map/ppermute | solution.py:260
  60.3 0.0 collective-permute-start.8
  60.3 0.0 collective-permute-done.11.refs_1_
  60.3 3.2 %collective-permute-start.12 = (bf16[256,256]{1,0:T(8,128)(2,1)S(1)}, bf16[256,256]{1,0:T(8,128)(2,1)S(1)}, u32[]{:S(2)}, u32[]{:S(2)}) collective-permute-start(bf16[256,256]{1,0:T(8,128)(2,1)S(1)} %collective-permute-done.11.refs_1_), channel_id=1, source_target_pairs={{0,28},{4,0},{8,4},{12,8},{16,12},{20,16},{24,20},{28,24},{1,29},{... | collective-permute-start | bytes 393224 | tf_op jit(solution)/shard_map/ppermute | solution.py:260
  63.6 2.9 %collective-permute-done.8.refs_1_ = bf16[256,256]{1,0:T(8,128)(2,1)S(1)} collective-permute-done((bf16[256,256]{1,0:T(8,128)(2,1)S(1)}, bf16[256,256]{1,0:T(8,128)(2,1)S(1)}, u32[]{:S(2)}, u32[]{:S(2)}) %collective-permute-start.8) | collective-permute-done | bytes 131104 | tf_op jit(solution)/shard_map/ppermute | solution.py:260
  66.5 0.0 collective-permute-start.9
  66.5 0.0 collective-permute-done.12.refs_2_
  66.5 6.2 %collective-permute-done.9.refs_0_ = bf16[256,256]{1,0:T(8,128)(2,1)S(1)} collective-permute-done((bf16[256,256]{1,0:T(8,128)(2,1)S(1)}, bf16[256,256]{1,0:T(8,128)(2,1)S(1)}, u32[]{:S(2)}, u32[]{:S(2)}) %collective-permute-start.9) | collective-permute-done | bytes 131104 | tf_op jit(solution)/shard_map/ppermute | solution.py:260
  72.7 4.2 %all-to-all-done.1.pay_ref = bf16[8,1040,128]{2,1,0:T(8,128)(2,1)S(1)} async-done(((bf16[8,1040,128]{2,1,0:T(8,128)(2,1)}), bf16[8,1040,128]{2,1,0:T(8,128)(2,1)S(1)}, u32[]{:S(2)}, u32[]{:S(2)}) %all-to-all-start.1) | async-done | bytes 2129952 | tf_op jit(solution)/shard_map/all_to_all | solution.py:287
  76.9 9.2 %far.1 = (bf16[8,256,128]{2,1,0:T(8,128)(2,1)S(1)}, f32[8,8,256]{2,1,0:T(8,128)S(1)}, f32[8,128,256]{2,1,0:T(8,128)S(1)}, bf16[2,256,128]{2,1,0:T(8,128)(2,1)S(1...) custom-call(bf16[8,1040,128]{2,1,0:T(8,128)(2,1)S(1)} %all-to-all-done.1.pay_ref, ...), custom_call_target="tpu_custom_call" | custom-call | flops 15032385536 | bytes 4194304 | tf_op jit(solution)/shard_map/far/pallas_call | solution.py:215
  86.1 1.7 %collective-permute-start.13 = (bf16[2,256,128]{2,1,0:T(8,128)(2,1)S(1)}, bf16[2,256,128]{2,1,0:T(8,128)(2,1)S(1)}, u32[]{:S(2)}, u32[]{:S(2)}) collective-permute-start(bf16[2,256,128]{2,1,0:T(8,128)(2,1)S(1)} %get-tuple-element.35), channel_id=1, source_target_pairs={{0,16},{4,20},{8,24},{12,28},{16,0},{20,4},{24,8},{28,12},{1,17},{... | collective-permute-start | bytes 393224 | tf_op jit(solution)/shard_map/ppermute | solution.py:260
  87.8 3.4 %collective-permute-start.14 = (bf16[2,256,128]{2,1,0:T(8,128)(2,1)S(1)}, bf16[2,256,128]{2,1,0:T(8,128)(2,1)S(1)}, u32[]{:S(2)}, u32[]{:S(2)}) collective-permute-start(bf16[2,256,128]{2,1,0:T(8,128)(2,1)S(1)} %get-tuple-element.36), channel_id=1, source_target_pairs={{0,20},{4,24},{8,28},{12,0},{16,4},{20,8},{24,12},{28,16},{1,21},{... | collective-permute-start | bytes 393224 | tf_op jit(solution)/shard_map/ppermute | solution.py:260
  91.2 0.4 collective-permute-start.15
  91.6 13.4 %near.1 = (bf16[8,128,256]{2,1,0:T(8,128)(2,1)}, bf16[2,256,128]{2,1,0:T(8,128)(2,1)S(1)}, bf16[2,256,128]{2,1,0:T(8,128)(2,1)S(1)}, bf16[2,256,128]{2,1,0:T(8,1...) custom-call(bf16[8,1040,128]{2,1,0:T(8,128)(2,1)S(1)} %all-to-all-done.1.pay_ref, ...), custom_call_target="tpu_custom_call" | custom-call | flops 15032385536 | bytes 4194304 | tf_op jit(solution)/shard_map/near/pallas_call | solution.py:215
  105.0 0.7 copy-done.3
  105.7 0.7 copy-done.4
  106.3 0.7 copy-done.5
  107.0 0.0 collective-permute-done.13.refs_0_
  107.0 0.0 collective-permute-done.14.refs_1_
  107.0 0.0 collective-permute-done.15.refs_2_
  107.0 7.3 %all-to-all-start.2 = ((bf16[8,128,256]{2,1,0:T(8,128)(2,1)}), bf16[8,128,256]{2,1,0:T(8,128)(2,1)S(1)}, u32[]{:S(2)}, u32[]{:S(2)}) async-start(bf16[8,128,256]{2,1,0:T(8,128)(2,1)} %get-tuple-element.50), calls=%async_computation.2 | async-start | bytes 1048576 | tf_op jit(solution)/shard_map/all_to_all | solution.py:293
  114.3 4.1 %collective-permute-start.16 = (bf16[2,256,128]{2,1,0:T(8,128)(2,1)}, bf16[2,256,128]{2,1,0:T(8,128)(2,1)S(1)}, u32[]{:S(2)}, u32[]{:S(2)}) collective-permute-start(bf16[2,256,128]{2,1,0:T(8,128)(2,1)} %copy-done.5), channel_id=1, source_target_pairs={{0,24},{4,28},{8,0},{12,4},{16,8},{20,12},{24,16},{28,20},{1,25},{... | collective-permute-start | bytes 393224 | tf_op jit(solution)/shard_map/ppermute | solution.py:260
  118.3 0.0 collective-permute-start.17
  118.3 3.4 %collective-permute-start.18 = (bf16[2,256,128]{2,1,0:T(8,128)(2,1)}, bf16[2,256,128]{2,1,0:T(8,128)(2,1)S(1)}, u32[]{:S(2)}, u32[]{:S(2)}) collective-permute-start(bf16[2,256,128]{2,1,0:T(8,128)(2,1)} %copy-done.3), channel_id=1, source_target_pairs={{0,28},{4,0},{8,4},{12,8},{16,12},{20,16},{24,20},{28,24},{1,29},{... | collective-permute-start | bytes 393224 | tf_op jit(solution)/shard_map/ppermute | solution.py:260
  121.7 0.0 collective-permute-start.19
  121.7 1.6 %collective-permute-done.16.refs_3_ = bf16[2,256,128]{2,1,0:T(8,128)(2,1)S(1)} collective-permute-done((bf16[2,256,128]{2,1,0:T(8,128)(2,1)}, bf16[2,256,128]{2,1,0:T(8,128)(2,1)S(1)}, u32[]{:S(2)}, u32[]{:S(2)}) %collective-permute-start.16) | collective-permute-done | bytes 131104 | tf_op jit(solution)/shard_map/ppermute | solution.py:260
  123.3 4.0 %collective-permute-done.17.refs_4_ = bf16[2,256,128]{2,1,0:T(8,128)(2,1)S(1)} collective-permute-done((bf16[2,256,128]{2,1,0:T(8,128)(2,1)}, bf16[2,256,128]{2,1,0:T(8,128)(2,1)S(1)}, u32[]{:S(2)}, u32[]{:S(2)}) %collective-permute-start.17) | collective-permute-done | bytes 131104 | tf_op jit(solution)/shard_map/ppermute | solution.py:260
  127.3 0.0 collective-permute-done.18.refs_5_
  127.3 1.3 collective-permute-done.19.refs_6_
  128.6 0.0 all-to-all-done.2.refs_8_
  128.6 0.9 finish.1
  (28 shorter events, 0.2 us)
Async XLA Ops:
  0.6 26.8 %copy-start.12 = (s32[1,64]{1,0:T(1,128)S(1)}, s32[1,64]{1,0:T(1,128)}, u32[]{:S(2)}) copy-start(s32[1,64]{1,0:T(1,128)} %param.19) | copy-start | bytes 772
  0.6 27.2 %copy-start.11 = (f32[2,256]{1,0:T(2,128)S(1)}, f32[2,256]{1,0:T(2,128)}, u32[]{:S(2)}) copy-start(f32[2,256]{1,0:T(2,128)} %param.14) | copy-start | bytes 6148
  0.7 39.2 %copy-start = (bf16[256,128]{1,0:T(8,128)(2,1)S(1)}, bf16[256,128]{1,0:T(8,128)(2,1)}, u32[]{:S(2)}) copy-start(bf16[256,128]{1,0:T(8,128)(2,1)} %q_ref.1) | copy-start | bytes 196612
  0.7 39.1 %copy-start.1 = (bf16[256,128]{1,0:T(8,128)(2,1)S(1)}, bf16[256,128]{1,0:T(8,128)(2,1)}, u32[]{:S(2)}) copy-start(bf16[256,128]{1,0:T(8,128)(2,1)} %out_ref.1) | copy-start | bytes 196612
  0.7 9.8 %collective-permute-start.1 = (bf16[128,1024]{1,0:T(8,128)(2,1)}, bf16[128,1024]{1,0:T(8,128)(2,1)S(1)}, u32[]{:S(2)}, u32[]{:S(2)}) collective-permute-start(bf16[128,1024]{1,0:T(8,128)(2,1)} %refs_3_.1), channel_id=1, source_target_pairs={{0,2},{2,0},{1,3},{3,1},{4,6},{6,4},{5,7},{7,5},{8,10},{10,8},{9,1... | collective-permute-start | bytes 786440 | tf_op jit(solution)/shard_map/ppermute | solution.py:256
  4.0 6.6 %collective-permute-start = (bf16[128,1024]{1,0:T(8,128)(2,1)}, bf16[128,1024]{1,0:T(8,128)(2,1)S(1)}, u32[]{:S(2)}, u32[]{:S(2)}) collective-permute-start(bf16[128,1024]{1,0:T(8,128)(2,1)} %refs_3_.1), channel_id=1, source_target_pairs={{0,1},{1,0},{2,3},{3,2},{4,5},{5,4},{6,7},{7,6},{8,9},{9,8},{10,11... | collective-permute-start | bytes 786440 | tf_op jit(solution)/shard_map/ppermute | solution.py:256
  10.5 1.5 %copy-start.6 = (bf16[128,1024]{1,0:T(8,128)(2,1)}, bf16[128,1024]{1,0:T(8,128)(2,1)S(1)}, u32[]{:S(2)}) copy-start(bf16[128,1024]{1,0:T(8,128)(2,1)S(1)} %collective-permute-done.1.refs_5_) | copy-start | bytes 786436
  10.5 1.5 %collective-permute-start.2 = (bf16[128,1024]{1,0:T(8,128)(2,1)S(1)}, bf16[128,1024]{1,0:T(8,128)(2,1)S(1)}, u32[]{:S(2)}, u32[]{:S(2)}) collective-permute-start(bf16[128,1024]{1,0:T(8,128)(2,1)S(1)} %collective-permute-done.1.refs_5_), channel_id=1, source_target_pairs={{0,1},{1,0},{2,3},{3,2},{4,5},{5,4},{6,7},{7,6},{8,9},{9,8},{10,11... | collective-permute-start | bytes 786440 | tf_op jit(solution)/shard_map/ppermute | solution.py:256
  10.5 1.5 %copy-start.7 = (bf16[128,1024]{1,0:T(8,128)(2,1)}, bf16[128,1024]{1,0:T(8,128)(2,1)S(1)}, u32[]{:S(2)}) copy-start(bf16[128,1024]{1,0:T(8,128)(2,1)S(1)} %collective-permute-done.refs_4_) | copy-start | bytes 786436
  12.1 0.7 copy-start.8
  15.9 23.9 %all-to-all-start = ((bf16[32,32,128]{2,1,0:T(8,128)(2,1)}), bf16[32,32,128]{2,1,0:T(8,128)(2,1)S(1)}, u32[]{:S(2)}, u32[]{:S(2)}) async-start(bf16[32,32,128]{2,1,0:T(8,128)(2,1)} %bitcast.4), calls=%async_computation | async-start | bytes 524288 | tf_op jit(solution)/shard_map/all_to_all | solution.py:272
  27.8 3.7 %collective-permute-start.3 = (bf16[256,128]{1,0:T(8,128)(2,1)}, bf16[256,128]{1,0:T(8,128)(2,1)S(1)}, u32[]{:S(2)}, u32[]{:S(2)}) collective-permute-start(bf16[256,128]{1,0:T(8,128)(2,1)} %get-tuple-element.29), channel_id=1, source_target_pairs={{0,1},{1,0},{2,3},{3,2},{4,5},{5,4},{6,7},{7,6},{8,9},{9,8},{10,11... | collective-permute-start | bytes 196616 | tf_op jit(solution)/shard_map/ppermute | solution.py:270
  28.2 7.1 %collective-permute-start.4 = (bf16[256,128]{1,0:T(8,128)(2,1)}, bf16[256,128]{1,0:T(8,128)(2,1)S(1)}, u32[]{:S(2)}, u32[]{:S(2)}) collective-permute-start(bf16[256,128]{1,0:T(8,128)(2,1)} %get-tuple-element.30), channel_id=1, source_target_pairs={{0,2},{1,3},{2,0},{3,1},{4,6},{5,7},{6,4},{7,5},{8,10},{9,11},{10,... | collective-permute-start | bytes 196616 | tf_op jit(solution)/shard_map/ppermute | solution.py:270
  31.4 7.3 %collective-permute-start.5 = (bf16[256,128]{1,0:T(8,128)(2,1)}, bf16[256,128]{1,0:T(8,128)(2,1)S(1)}, u32[]{:S(2)}, u32[]{:S(2)}) collective-permute-start(bf16[256,128]{1,0:T(8,128)(2,1)} %get-tuple-element.31), channel_id=1, source_target_pairs={{0,3},{1,2},{2,1},{3,0},{4,7},{5,6},{6,5},{7,4},{8,11},{9,10},{10,... | collective-permute-start | bytes 196616 | tf_op jit(solution)/shard_map/ppermute | solution.py:270
  39.8 0.8 copy-start.2
  42.3 5.1 %copy-start.9 = (bf16[256,128]{1,0:T(8,128)(2,1)S(1)}, bf16[256,128]{1,0:T(8,128)(2,1)}, u32[]{:S(2)}) copy-start(bf16[256,128]{1,0:T(8,128)(2,1)} %param.11) | copy-start | bytes 196612
  42.3 5.1 %copy-start.10 = (bf16[256,128]{1,0:T(8,128)(2,1)S(1)}, bf16[256,128]{1,0:T(8,128)(2,1)}, u32[]{:S(2)}) copy-start(bf16[256,128]{1,0:T(8,128)(2,1)} %param.12) | copy-start | bytes 196612
  42.3 34.6 %all-to-all-start.1 = ((bf16[8,1040,128]{2,1,0:T(8,128)(2,1)}), bf16[8,1040,128]{2,1,0:T(8,128)(2,1)S(1)}, u32[]{:S(2)}, u32[]{:S(2)}) async-start(bf16[8,1040,128]{2,1,0:T(8,128)(2,1)} %pack.1), calls=%async_computation.1 | async-start | bytes 4259840 | tf_op jit(solution)/shard_map/all_to_all | solution.py:287
  47.5 6.7 %collective-permute-start.6 = (bf16[256,256]{1,0:T(8,128)(2,1)S(1)}, bf16[256,256]{1,0:T(8,128)(2,1)S(1)}, u32[]{:S(2)}, u32[]{:S(2)}) collective-permute-start(bf16[256,256]{1,0:T(8,128)(2,1)S(1)} %constant_dynamic-update-slice_fusion.refs_4_), channel_id=1, source_target_pairs={{0,4},{4,8},{8,12},{12,16},{16,20},{20,24},{24,28},{28,0},{1,5},{5... | collective-permute-start | bytes 393224 | tf_op jit(solution)/shard_map/ppermute | solution.py:260
  50.0 5.0 %collective-permute-start.10 = (bf16[256,256]{1,0:T(8,128)(2,1)S(1)}, bf16[256,256]{1,0:T(8,128)(2,1)S(1)}, u32[]{:S(2)}, u32[]{:S(2)}) collective-permute-start(bf16[256,256]{1,0:T(8,128)(2,1)S(1)} %constant_dynamic-update-slice_fusion.refs_4_), channel_id=1, source_target_pairs={{0,28},{4,0},{8,4},{12,8},{16,12},{20,16},{24,20},{28,24},{1,29},{... | collective-permute-start | bytes 393224 | tf_op jit(solution)/shard_map/ppermute | solution.py:260
  54.1 6.2 %collective-permute-start.7 = (bf16[256,256]{1,0:T(8,128)(2,1)S(1)}, bf16[256,256]{1,0:T(8,128)(2,1)S(1)}, u32[]{:S(2)}, u32[]{:S(2)}) collective-permute-start(bf16[256,256]{1,0:T(8,128)(2,1)S(1)} %collective-permute-done.6.refs_2_), channel_id=1, source_target_pairs={{0,4},{4,8},{8,12},{12,16},{16,20},{20,24},{24,28},{28,0},{1,5},{5... | collective-permute-start | bytes 393224 | tf_op jit(solution)/shard_map/ppermute | solution.py:260
  55.0 5.4 %collective-permute-start.11 = (bf16[256,256]{1,0:T(8,128)(2,1)S(1)}, bf16[256,256]{1,0:T(8,128)(2,1)S(1)}, u32[]{:S(2)}, u32[]{:S(2)}) collective-permute-start(bf16[256,256]{1,0:T(8,128)(2,1)S(1)} %collective-permute-done.10.refs_3_), channel_id=1, source_target_pairs={{0,28},{4,0},{8,4},{12,8},{16,12},{20,16},{24,20},{28,24},{1,29},{... | collective-permute-start | bytes 393224 | tf_op jit(solution)/shard_map/ppermute | solution.py:260
  60.3 6.2 %collective-permute-start.8 = (bf16[256,256]{1,0:T(8,128)(2,1)S(1)}, bf16[256,256]{1,0:T(8,128)(2,1)S(1)}, u32[]{:S(2)}, u32[]{:S(2)}) collective-permute-start(bf16[256,256]{1,0:T(8,128)(2,1)S(1)} %collective-permute-done.7.refs_0_), channel_id=1, source_target_pairs={{0,4},{4,8},{8,12},{12,16},{16,20},{20,24},{24,28},{28,0},{1,5},{5... | collective-permute-start | bytes 393224 | tf_op jit(solution)/shard_map/ppermute | solution.py:260
  60.3 6.2 %collective-permute-start.12 = (bf16[256,256]{1,0:T(8,128)(2,1)S(1)}, bf16[256,256]{1,0:T(8,128)(2,1)S(1)}, u32[]{:S(2)}, u32[]{:S(2)}) collective-permute-start(bf16[256,256]{1,0:T(8,128)(2,1)S(1)} %collective-permute-done.11.refs_1_), channel_id=1, source_target_pairs={{0,28},{4,0},{8,4},{12,8},{16,12},{20,16},{24,20},{28,24},{1,29},{... | collective-permute-start | bytes 393224 | tf_op jit(solution)/shard_map/ppermute | solution.py:260
  66.5 6.2 %collective-permute-start.9 = (bf16[256,256]{1,0:T(8,128)(2,1)S(1)}, bf16[256,256]{1,0:T(8,128)(2,1)S(1)}, u32[]{:S(2)}, u32[]{:S(2)}) collective-permute-start(bf16[256,256]{1,0:T(8,128)(2,1)S(1)} %collective-permute-done.8.refs_1_), channel_id=1, source_target_pairs={{0,4},{4,8},{8,12},{12,16},{16,20},{20,24},{24,28},{28,0},{1,5},{5... | collective-permute-start | bytes 393224 | tf_op jit(solution)/shard_map/ppermute | solution.py:260
  86.1 20.9 %collective-permute-start.13 = (bf16[2,256,128]{2,1,0:T(8,128)(2,1)S(1)}, bf16[2,256,128]{2,1,0:T(8,128)(2,1)S(1)}, u32[]{:S(2)}, u32[]{:S(2)}) collective-permute-start(bf16[2,256,128]{2,1,0:T(8,128)(2,1)S(1)} %get-tuple-element.35), channel_id=1, source_target_pairs={{0,16},{4,20},{8,24},{12,28},{16,0},{20,4},{24,8},{28,12},{1,17},{... | collective-permute-start | bytes 393224 | tf_op jit(solution)/shard_map/ppermute | solution.py:260
  87.8 19.2 %collective-permute-start.14 = (bf16[2,256,128]{2,1,0:T(8,128)(2,1)S(1)}, bf16[2,256,128]{2,1,0:T(8,128)(2,1)S(1)}, u32[]{:S(2)}, u32[]{:S(2)}) collective-permute-start(bf16[2,256,128]{2,1,0:T(8,128)(2,1)S(1)} %get-tuple-element.36), channel_id=1, source_target_pairs={{0,20},{4,24},{8,28},{12,0},{16,4},{20,8},{24,12},{28,16},{1,21},{... | collective-permute-start | bytes 393224 | tf_op jit(solution)/shard_map/ppermute | solution.py:260
  91.2 15.8 %collective-permute-start.15 = (bf16[2,256,128]{2,1,0:T(8,128)(2,1)S(1)}, bf16[2,256,128]{2,1,0:T(8,128)(2,1)S(1)}, u32[]{:S(2)}, u32[]{:S(2)}) collective-permute-start(bf16[2,256,128]{2,1,0:T(8,128)(2,1)S(1)} %get-tuple-element.37), channel_id=1, source_target_pairs={{0,12},{4,16},{8,20},{12,24},{16,28},{20,0},{24,4},{28,8},{1,13},{... | collective-permute-start | bytes 393224 | tf_op jit(solution)/shard_map/ppermute | solution.py:260
  105.0 0.7 copy-start.3
  105.7 0.7 copy-start.4
  106.3 0.7 copy-start.5
  107.0 21.6 %all-to-all-start.2 = ((bf16[8,128,256]{2,1,0:T(8,128)(2,1)}), bf16[8,128,256]{2,1,0:T(8,128)(2,1)S(1)}, u32[]{:S(2)}, u32[]{:S(2)}) async-start(bf16[8,128,256]{2,1,0:T(8,128)(2,1)} %get-tuple-element.50), calls=%async_computation.2 | async-start | bytes 1048576 | tf_op jit(solution)/shard_map/all_to_all | solution.py:293
  114.3 9.1 %collective-permute-start.16 = (bf16[2,256,128]{2,1,0:T(8,128)(2,1)}, bf16[2,256,128]{2,1,0:T(8,128)(2,1)S(1)}, u32[]{:S(2)}, u32[]{:S(2)}) collective-permute-start(bf16[2,256,128]{2,1,0:T(8,128)(2,1)} %copy-done.5), channel_id=1, source_target_pairs={{0,24},{4,28},{8,0},{12,4},{16,8},{20,12},{24,16},{28,20},{1,25},{... | collective-permute-start | bytes 393224 | tf_op jit(solution)/shard_map/ppermute | solution.py:260
  118.3 9.0 %collective-permute-start.17 = (bf16[2,256,128]{2,1,0:T(8,128)(2,1)}, bf16[2,256,128]{2,1,0:T(8,128)(2,1)S(1)}, u32[]{:S(2)}, u32[]{:S(2)}) collective-permute-start(bf16[2,256,128]{2,1,0:T(8,128)(2,1)} %copy-done.4), channel_id=1, source_target_pairs={{0,8},{4,12},{8,16},{12,20},{16,24},{20,28},{24,0},{28,4},{1,9},{5... | collective-permute-start | bytes 393224 | tf_op jit(solution)/shard_map/ppermute | solution.py:260
  118.3 9.0 %collective-permute-start.18 = (bf16[2,256,128]{2,1,0:T(8,128)(2,1)}, bf16[2,256,128]{2,1,0:T(8,128)(2,1)S(1)}, u32[]{:S(2)}, u32[]{:S(2)}) collective-permute-start(bf16[2,256,128]{2,1,0:T(8,128)(2,1)} %copy-done.3), channel_id=1, source_target_pairs={{0,28},{4,0},{8,4},{12,8},{16,12},{20,16},{24,20},{28,24},{1,29},{... | collective-permute-start | bytes 393224 | tf_op jit(solution)/shard_map/ppermute | solution.py:260
  121.7 6.9 %collective-permute-start.19 = (bf16[2,256,128]{2,1,0:T(8,128)(2,1)S(1)}, bf16[2,256,128]{2,1,0:T(8,128)(2,1)S(1)}, u32[]{:S(2)}, u32[]{:S(2)}) collective-permute-start(bf16[2,256,128]{2,1,0:T(8,128)(2,1)S(1)} %get-tuple-element.48), channel_id=1, source_target_pairs={{0,4},{4,8},{8,12},{12,16},{16,20},{20,24},{24,28},{28,0},{1,5},{5... | collective-permute-start | bytes 393224 | tf_op jit(solution)/shard_map/ppermute | solution.py:260
